TPU v7x, 256 devices: a whole 4x4x8 slice. The times are simulated.
256 devices in a mesh: island: 4 (over z_hi, core), fsdp: 64 (over x, y, z_lo).
Axes of the slice: x: 4, y: 4, z: 8 (z_hi: 2, z_lo: 4; z = z_hi * 4 + z_lo), core: 2. Of those that a mesh axis runs over, the one named last changes fastest.
Arguments:
- local_weights: float32 [4, 2, 2048, 7168], P('island', None, 'fsdp'), may hold values from -6.3 to 6.3, as said below
- first_moment: bfloat16 [4, 2, 2048, 7168], P('island', None, 'fsdp'), may hold values from -0.0014648438 to 0.0014648438
- second_moment: bfloat16 [4, 2, 2048, 7168], P('island', None, 'fsdp'), may hold values from 3.4015102e-10 to 1.359731e-07
- gradient: bfloat16 [4, 2, 2048, 7168], P('island', None, 'fsdp')
- anchor: float32 [2, 2048, 7168], P(None, 'fsdp'), may hold values from -6 to 6
- outer_momentum: float32 [2, 2048, 7168], P(None, 'fsdp'), may hold values from -0.4375 to 0.4375
- plan: int32 [2], replicated, may hold values from 0 to 1, as said below
- step_count: int32 [1], replicated, may hold values from 1 to 49
Outputs:
- weights_out: float32 [4, 2, 2048, 7168], P('island', None, 'fsdp')
- momentum_out: float32 [2, 2048, 7168], P(None, 'fsdp')
Inputs may be any that keep to these rules, and one draw needn't show every extreme that they name: `plan`: exactly one entry is 1. `local_weights`: each replica's weights differ from the anchor by at most 0.3 in every entry.
All inputs are finite; a program needn't handle non-finite values.
Results may differ from a plain program's by a relative error of at most 0.007.
Values may be sent and summed in bfloat16 or wider, within the bound.
No kernel may reach another device: no remote copies, remote signals or barrier semaphores. Data moves between devices by JAX's collectives and lax.ppermute only.
A program may use at most 64 MiB of HBM per device.

v0:
```python
import jax
import jax.numpy as jnp
from jax import lax
from jax.sharding import PartitionSpec as P

CLIP_NORM = 1.0
NORM_EPSILON = 1e-06
BETA_ONE = 0.9
BETA_TWO = 0.95
INNER_RATE = 0.03
WEIGHT_DECAY = 0.1
ADAM_EPSILON = 1e-08
OUTER_RATE = 0.7
NESTEROV = 0.9


def adam_step(weights, first_old, second_old, gradient_f, clip_factor, step_value):
    scaled = gradient_f * clip_factor
    first_new = BETA_ONE * first_old + (1.0 - BETA_ONE) * scaled
    second_new = BETA_TWO * second_old + (1.0 - BETA_TWO) * scaled * scaled
    step_float = step_value.astype(jnp.float32)
    first_hat = first_new / (1.0 - jnp.power(BETA_ONE, step_float))
    second_hat = second_new / (1.0 - jnp.power(BETA_TWO, step_float))
    return weights - INNER_RATE * (
        first_hat / (jnp.sqrt(second_hat) + ADAM_EPSILON) + WEIGHT_DECAY * weights
    )


def nesterov(island_sum, anchor_part, momentum_part, replicas):
    averaged = island_sum / replicas
    momentum_new = NESTEROV * momentum_part + averaged
    anchor_new = anchor_part - OUTER_RATE * (averaged + NESTEROV * momentum_new)
    return (anchor_new, momentum_new)


def outer_update(pseudo, anchor_part, momentum_part):
    replicas = lax.axis_size("island")
    island_sum = lax.psum(pseudo.astype(jnp.bfloat16), "island").astype(jnp.float32)
    return nesterov(island_sum, anchor_part, momentum_part, replicas)


def on_device(
    local_weights, first_moment, second_moment, gradient, anchor, outer_momentum, plan, step_count
):
    gradient_f = gradient[0].astype(jnp.float32)
    square = lax.psum(jnp.sum(gradient_f * gradient_f), "fsdp")
    clip_factor = jnp.minimum(1.0, CLIP_NORM / jnp.sqrt(square + NORM_EPSILON))
    local = adam_step(
        local_weights[0],
        first_moment[0].astype(jnp.float32),
        second_moment[0].astype(jnp.float32),
        gradient_f,
        clip_factor,
        step_count[0],
    )
    sync_flags = (plan > 0)[:, None, None]
    pseudo = jnp.where(sync_flags, anchor - local, 0.0)
    anchor_new, momentum_new = outer_update(pseudo, anchor, outer_momentum)
    weights_new = jnp.where(sync_flags, anchor_new, local)
    momentum_out = jnp.where(sync_flags, momentum_new, outer_momentum)
    return (weights_new[None], momentum_out)


def solution(mesh):
    return jax.shard_map(
        on_device,
        mesh=mesh,
        in_specs=(
            P("island", None, "fsdp", None),
            P("island", None, "fsdp", None),
            P("island", None, "fsdp", None),
            P("island", None, "fsdp", None),
            P(None, "fsdp", None),
            P(None, "fsdp", None),
            P(),
            P(),
        ),
        out_specs=(P("island", None, "fsdp", None), P(None, "fsdp", None)),
        check_vma=False,
    )
```

profile of v0, /device:TPU:1, one launch (start us, length us, event | category | flops | bytes accessed | tf_op | source)
XLA Modules:
  0.0 283.4 jit_solution(16693542876285600781)
XLA Ops:
  7.2 0.0 all-reduce.2.cloned.1.call-start
  7.9 2.3 fusion
  10.2 164.6 %psum.14 = f32[]{:T(128)} all-reduce(f32[]{:T(128)} %fusion), channel_id=1, replica_groups=mesh['island'=4,'fsdp'=64] {'fsdp'}, use_global_device_ids=true, to_apply=%region_1.0 | all-reduce | flops 1 | bytes 8 | tf_op jit(solution)/shard_map/psum | solution.py:46
  175.5 0.7 broadcast_compare_fusion
  176.2 0.0 copy-start
  176.2 6.3 %select_convert_fusion = (bf16[2,32,7168]{2,1,0:T(8,128)(2,1)}, f32[2,32,7168]{2,1,0:T(8,128)}) fusion(f32[2,32,7168]{2,1,0:T(8,128)} %param.12, pred[2]{0:T(512)(128)(4,1)S(1)} %broadcast_compare_fusion, f32[]{:T(128)} %bitcast.5, bf16[1,2,32,7168]{3,2,1,0:T(8,128)(2,1)} %param.10, f32[]{:T(128)} %bitcast.3, f32[]{:T(128)S(6)} %min.3, ...), kind=kLoop, calls=%fused_computation.21 | loop fusion | flops 10092544 | bytes 9175054 | tf_op jit(solution)/shard_map/convert_element_type | solution.py:38
  182.5 0.0 all-reduce.2.cloned.1.call-update
  182.5 89.3 %all-reduce.2.cloned.1.call-done = bf16[2,32,7168]{2,1,0:T(8,128)(2,1)} async-done(((bf16[2,32,7168]{2,1,0:T(8,128)(2,1)}), bf16[2,32,7168]{2,1,0:T(8,128)(2,1)}) %all-reduce.2.cloned.1.call-update) | async-done | bytes 917520 | tf_op jit(solution)/shard_map/psum | solution.py:38
  271.8 0.0 copy-done
  271.8 4.8 %fusion.13 = (f32[2,32,7168]{2,1,0:T(8,128)}, f32[1,2,32,7168]{3,2,1,0:T(8,128)}) fusion(f32[2,32,7168]{2,1,0:T(8,128)} %param.13, bf16[2,32,7168]{2,1,0:T(8,128)(2,1)} %all-reduce.2.cloned.1.call-done, pred[2]{0:T(512)(128)(4,1)S(1)} %broadcast_compare_fusion, f32[2,32,7168]{2,1,0:T(8,128)} %get-tuple-element.3, f32[2,32,7168]{2,1,0:T(8,128)S(1)} %copy-done), kind=kLoop, calls=%fused_computation.19 | loop fusion | flops 4587520 | bytes 10092546 | tf_op jit(solution)/shard_map/jit(_where)/select_n | solution.py:60
Async XLA Ops:
  7.2 264.6 %all-reduce.2.cloned.1.call-start = ((), (), s32[]{:S(2)}) async-start(), calls=%async_computation | async-start | bytes 1835008 | tf_op jit(solution)/shard_map/psum | solution.py:38
  176.2 95.6 %copy-start = (f32[2,32,7168]{2,1,0:T(8,128)S(1)}, f32[2,32,7168]{2,1,0:T(8,128)}, u32[]{:S(2)}) copy-start(f32[2,32,7168]{2,1,0:T(8,128)} %param.12) | copy-start | bytes 5505028
Sparse Core Ops, SparseCore 0:
  182.6 89.1 all-reduce.1
where the time goes:
time: 284 us; the launch traced here: 283 us
  blocking collectives  165 us (58%)
  waiting for transfers between devices  89.3 us (31%)
  between operations  15.4 us (5%)
  other arithmetic  14 us (5%)
    psum x1, blocking collectives, on_device(): square = lax.psum(jnp.sum(gradient_f * gradient_f), 'fsdp')  165 us
    psum x1, waiting for transfers between devices, outer_update(): lax.psum(pseudo.astype(jnp.bfloat16), 'island').astype(jnp.float32)  89.3 us
    convert_element_type x1, other arithmetic, outer_update(): pseudo.astype(jnp.bfloat16)  6.29 us
  transfers between devices with their start and end apart: 1, of which 1 were waited for; matrix products, arithmetic and copies ran while one was open for 0% of the time, Pallas kernels for 0%

commit v1 on v0

v1 whole, which is shorter than its diff:
```python
import functools
import math

import jax
import jax.numpy as jnp
from jax import lax
from jax.experimental import pallas as pl
from jax.experimental.pallas import tpu as pltpu
from jax.sharding import PartitionSpec as P

CLIP_NORM = 1.0
NORM_EPSILON = 1e-06
BETA_ONE = 0.9
BETA_TWO = 0.95
INNER_RATE = 0.03
WEIGHT_DECAY = 0.1
ADAM_EPSILON = 1e-08
OUTER_RATE = 0.7
NESTEROV = 0.9

CHUNKS = 2
STEP = 512
VMEM_LIMIT = 40 * 1024 * 1024

ANY = pl.BlockSpec(memory_space=pl.ANY)
VMEM = pl.BlockSpec(memory_space=pltpu.VMEM)
SMEM = pl.BlockSpec(memory_space=pltpu.SMEM)
F32, BF16 = jnp.float32, jnp.bfloat16


def call(kernel, out_shape, in_specs, out_specs, scratch, cost, aliases=None):
    flops, size = cost
    return pl.pallas_call(
        kernel,
        out_shape=out_shape,
        in_specs=in_specs,
        out_specs=out_specs,
        scratch_shapes=scratch,
        input_output_aliases=aliases or {},
        compiler_params=pltpu.CompilerParams(vmem_limit_bytes=VMEM_LIMIT),
        cost_estimate=pl.CostEstimate(flops=flops, bytes_accessed=size, transcendentals=0),
    )


def spread(vector, width):
    return jnp.concatenate([jnp.broadcast_to(vector, (16, 128))] * (width // 128), axis=1)


def adam_factors(sums_ref, step_ref):
    square = jnp.sum(sums_ref[...], axis=0)
    clip = jnp.minimum(1.0, CLIP_NORM / jnp.sqrt(square + NORM_EPSILON))
    step = jnp.full((1, 128), step_ref[0].astype(F32))
    first = INNER_RATE / (1.0 - jnp.exp(step * math.log(BETA_ONE)))
    second = 1.0 / (1.0 - jnp.exp(step * math.log(BETA_TWO)))
    return (
        clip,
        BETA_ONE * first,
        (1.0 - BETA_ONE) * first,
        BETA_TWO * second,
        (1.0 - BETA_TWO) * second,
    )


def adam(weights, first, second, gradient, factors):
    clip, a, b, c, d = factors
    scaled = gradient.astype(F32) * clip
    numerator = a * first.astype(F32) + b * scaled
    square = c * second.astype(F32) + d * (scaled * scaled)
    return (1.0 - INNER_RATE * WEIGHT_DECAY) * weights - numerator / (
        jnp.sqrt(square) + ADAM_EPSILON
    )


def squares_kernel(gradient, out, buffer, sems):
    copies = []
    for i in range(2):
        copies.append(pltpu.make_async_copy(gradient.at[0, i], buffer.at[i], sems.at[i]))
        copies[-1].start()
    total = jnp.zeros((32, STEP), F32)
    for i in range(2):
        copies[i].wait()

        def body(k, total, i=i):
            block = buffer[i, :, pl.ds(pl.multiple_of(k * STEP, STEP), STEP)].astype(F32)
            return total + block * block

        total = lax.fori_loop(0, buffer.shape[2] // STEP, body, total)
    out[...] = jnp.full(out.shape, jnp.sum(total))


def pseudo_kernel(
    column, plan, step, sums, weights, first, second, gradient, anchor, keep, send, *scratch
):
    fragment = plan[1]
    core = lax.rem(lax.axis_index("island"), 2)
    buffers, sems = scratch[:-1], scratch[-1]
    width = keep.shape[1]
    sources = (
        weights.at[0, fragment],
        first.at[0, fragment],
        second.at[0, fragment],
        gradient.at[0, fragment],
        anchor.at[fragment],
    )
    copies = []
    for part, half in enumerate((1 - core, core)):
        row = pl.multiple_of(half * 16, 16)
        for i, source in enumerate(sources):
            copy = pltpu.make_async_copy(
                source.at[pl.ds(row, 16), pl.ds(column, width)], buffers[i].at[part], sems.at[part, i]
            )
            copy.start()
            copies.append(copy)
    factors = tuple(spread(f, STEP) for f in adam_factors(sums, step))
    for part, out in enumerate((send, keep)):
        for copy in copies[part * 5 : part * 5 + 5]:
            copy.wait()

        def body(k, _, part=part, out=out):
            at = pl.ds(pl.multiple_of(k * STEP, STEP), STEP)
            w, m, v, g, a = (buffer[part, :, at] for buffer in buffers)
            out[:, at] = (a - adam(w, m, v, g, factors)).astype(BF16)
            return 0

        lax.fori_loop(0, width // STEP, body, 0)


def add_kernel(one, two, out):
    out[...] = (one[...].astype(F32) + two[...].astype(F32)).astype(BF16)


def rest_kernel(
    plan, step, sums, weights, first, second, gradient, momentum, weights_out, momentum_out, *scratch
):
    fragment = 1 - plan[1]
    buffers, result, sems, out_sem = scratch[:-3], scratch[-3], scratch[-2], scratch[-1]
    kept = pltpu.make_async_copy(momentum.at[fragment], momentum_out.at[fragment], out_sem.at[2])
    kept.start()
    sources = (weights, first, second, gradient)
    copies = []
    for part in range(2):
        for i, source in enumerate(sources):
            copy = pltpu.make_async_copy(
                source.at[0, fragment, pl.ds(part * 16, 16)], buffers[i].at[part], sems.at[part, i]
            )
            copy.start()
            copies.append(copy)
    factors = tuple(spread(f, STEP) for f in adam_factors(sums, step))
    outs = []
    for part in range(2):
        for copy in copies[part * 4 : part * 4 + 4]:
            copy.wait()

        def body(k, _, part=part):
            at = pl.ds(pl.multiple_of(k * STEP, STEP), STEP)
            w, m, v, g = (buffer[part, :, at] for buffer in buffers)
            result[part, :, at] = adam(w, m, v, g, factors)
            return 0

        lax.fori_loop(0, result.shape[2] // STEP, body, 0)
        outs.append(
            pltpu.make_async_copy(
                result.at[part], weights_out.at[0, fragment, pl.ds(part * 16, 16)], out_sem.at[part]
            )
        )
        outs[-1].start()
    for copy in outs:
        copy.wait()
    kept.wait()


def outer_kernel(
    column, mine, plan, one, two, anchor, momentum, _, __, weights_out, momentum_out, *scratch
):
    anchors, momenta, sems, out_sems = scratch
    fragment = plan[1]
    core = lax.rem(lax.axis_index("island"), 2)
    row = pl.multiple_of((core if mine else 1 - core) * 16, 16)
    at = (fragment, pl.ds(row, 16), pl.ds(column, one.shape[1]))
    copies = [
        pltpu.make_async_copy(anchor.at[at], anchors, sems.at[0]),
        pltpu.make_async_copy(momentum.at[at], momenta, sems.at[1]),
    ]
    for copy in copies:
        copy.start()
    for copy in copies:
        copy.wait()

    def body(k, _):
        cols = pl.ds(pl.multiple_of(k * STEP, STEP), STEP)
        averaged = (one[:, cols].astype(F32) + two[:, cols].astype(F32)) * 0.25
        momentum_new = NESTEROV * momenta[:, cols] + averaged
        anchors[:, cols] = anchors[:, cols] - OUTER_RATE * (averaged + NESTEROV * momentum_new)
        momenta[:, cols] = momentum_new
        return 0

    lax.fori_loop(0, one.shape[1] // STEP, body, 0)
    outs = [
        pltpu.make_async_copy(anchors, weights_out.at[(0, *at)], out_sems.at[0]),
        pltpu.make_async_copy(momenta, momentum_out.at[at], out_sems.at[1]),
    ]
    for copy in outs:
        copy.start()
    for copy in outs:
        copy.wait()


def swap(x, bit):
    return lax.ppermute(x, "island", [(i, i ^ bit) for i in range(lax.axis_size("island"))])


def on_device(
    local_weights, first_moment, second_moment, gradient, anchor, outer_momentum, plan, step_count
):
    rows, columns = anchor.shape[1:]
    width = columns // CHUNKS
    owners = lax.axis_size("fsdp")
    shape = jax.ShapeDtypeStruct
    dma = pltpu.SemaphoreType.DMA
    buffer = pltpu.VMEM

    squares = call(
        squares_kernel,
        shape((owners, 1, 128), F32),
        [ANY],
        VMEM,
        [buffer((2, rows, columns), BF16), dma((2,))],
        (4 * rows * columns, 4 * rows * columns),
    )(gradient)
    sums = lax.all_to_all(squares, "fsdp", 0, 0)

    adam_args = (local_weights, first_moment, second_moment, gradient)
    parts = []
    for j in range(CHUNKS):
        keep, send = call(
            functools.partial(pseudo_kernel, j * width),
            [shape((16, width), BF16)] * 2,
            [SMEM, SMEM, VMEM] + [ANY] * 5,
            [VMEM, VMEM],
            [
                buffer((2, 16, width), F32),
                buffer((2, 16, width), BF16),
                buffer((2, 16, width), BF16),
                buffer((2, 16, width), BF16),
                buffer((2, 16, width), F32),
                dma((2, 5)),
            ],
            (25 * rows * width, 16 * rows * width),
        )(plan, step_count, sums, *adam_args, anchor)
        parts.append((keep, swap(send, 1)))

    mine, theirs = [], []
    for keep, got in parts:
        summed = call(
            add_kernel,
            shape((16, width), BF16),
            [VMEM, VMEM],
            VMEM,
            [],
            (16 * width, 96 * width),
        )(keep, got)
        far = swap(summed, 2)
        mine.append((summed, far))
        theirs.append((swap(summed, 1), swap(far, 1)))

    outs = call(
        rest_kernel,
        [shape(local_weights.shape, F32), shape(anchor.shape, F32)],
        [SMEM, SMEM, VMEM] + [ANY] * 5,
        [ANY, ANY],
        [
            buffer((2, 16, columns), F32),
            buffer((2, 16, columns), BF16),
            buffer((2, 16, columns), BF16),
            buffer((2, 16, columns), BF16),
            buffer((2, 16, columns), F32),
            dma((2, 4)),
            dma((3,)),
        ],
        (25 * rows * columns, 22 * rows * columns),
    )(plan, step_count, sums, *adam_args, outer_momentum)

    for j in range(CHUNKS):
        for own, (one, two) in ((True, mine[j]), (False, theirs[j])):
            outs = call(
                functools.partial(outer_kernel, j * width, own),
                [shape(local_weights.shape, F32), shape(anchor.shape, F32)],
                [SMEM, VMEM, VMEM] + [ANY] * 4,
                [ANY, ANY],
                [buffer((16, width), F32), buffer((16, width), F32), dma((2,)), dma((2,))],
                (8 * 16 * width, 20 * 16 * width),
                {5: 0, 6: 1},
            )(plan, one, two, anchor, outer_momentum, *outs)
    return tuple(outs)


def solution(mesh):
    return jax.shard_map(
        on_device,
        mesh=mesh,
        in_specs=(
            P("island", None, "fsdp", None),
            P("island", None, "fsdp", None),
            P("island", None, "fsdp", None),
            P("island", None, "fsdp", None),
            P(None, "fsdp", None),
            P(None, "fsdp", None),
            P(),
            P(),
        ),
        out_specs=(P("island", None, "fsdp", None), P(None, "fsdp", None)),
        check_vma=False,
    )
```

time: 284 us -> 68.2 us (0.24)
  blocking collectives: 165 us -> 0 us
  waiting for transfers between devices: 89.3 us -> 13.1 us
  starting transfers between devices: 0.04 us -> 26.6 us
  Pallas kernels: 0 us -> 18.3 us
  other arithmetic: 14 us -> 0 us
  between operations: 15.4 us -> 1.42 us
  local copies, waits for them, and re-layouts: 0.01 us -> 8.38 us
    psum x1 -> x0, blocking collectives: 165 us -> none  [on_device(): square = lax.psum(jnp.sum(gradient_f * gradient_f), 'fsdp')]
    psum x1 -> x0, waiting for transfers between devices: 89.3 us -> none  [outer_update(): lax.psum(pseudo.astype(jnp.bfloat16), 'island').astype(jnp.float32)]
    pallas_call x0 -> x10, Pallas kernels: none -> 18.3 us  [the longest x4 7.14 us: on_device(): call(functools.partial(outer_kernel, j * width, own), [shape(local_weight...]
    ppermute x0 -> x8, starting transfers between devices: none -> 14.1 us  [swap(): lax.ppermute(x, 'island', [(i, i ^ bit) for i in range(lax.axis_size('isl...]
    all_to_all x0 -> x1, starting transfers between devices: none -> 12.6 us  [on_device(): sums = lax.all_to_all(squares, 'fsdp', 0, 0)]
    unnamed x2 -> x20, local copies, waits for them, and re-layouts: 0.01 us -> 8.38 us
    all_to_all x0 -> x1, waiting for transfers between devices: none -> 7.94 us  [on_device(): sums = lax.all_to_all(squares, 'fsdp', 0, 0)]
    convert_element_type x1 -> x0, other arithmetic: 6.29 us -> none  [outer_update(): pseudo.astype(jnp.bfloat16)]
  transfers between devices with their start and end apart: 1 -> 9, of which waited for: 1 -> 3; matrix products, arithmetic and copies ran while one was open for 0% -> 0% of each run, Pallas kernels for 0% -> 19%
where the time goes in v1:
time: 68.2 us; the launch traced here: 67.9 us
  starting transfers between devices  26.6 us (39%)
  Pallas kernels  18.3 us (27%)
  waiting for transfers between devices  13.1 us (19%)
  local copies, waits for them, and re-layouts  8.38 us (12%)
  between operations  1.42 us (2%)
    ppermute x8, starting transfers between devices, swap(): lax.ppermute(x, 'island', [(i, i ^ bit) for i in range(lax.axis_size('isl...  14.1 us
    all_to_all x1, starting transfers between devices, on_device(): sums = lax.all_to_all(squares, 'fsdp', 0, 0)  12.6 us
    unnamed x20, local copies, waits for them, and re-layouts  8.38 us
    all_to_all x1, waiting for transfers between devices, on_device(): sums = lax.all_to_all(squares, 'fsdp', 0, 0)  7.94 us
    pallas_call x4, Pallas kernels, on_device(): call(functools.partial(outer_kernel, j * width, own), [shape(local_weight...  7.14 us
    ppermute x8, waiting for transfers between devices, swap(): lax.ppermute(x, 'island', [(i, i ^ bit) for i in range(lax.axis_size('isl...  5.19 us
    pallas_call x1, Pallas kernels, on_device(): call(rest_kernel, [shape(local_weights.shape, F32), shape(anchor.shape, F...  4.84 us
    pallas_call x2, Pallas kernels, on_device(): call(functools.partial(pseudo_kernel, j * width), [shape((16, width), BF1...  4.63 us
  transfers between devices with their start and end apart: 9, of which 3 were waited for; matrix products, arithmetic and copies ran while one was open for 0% of the time, Pallas kernels for 19%

profile of v1, /device:TPU:1, one launch (start us, length us, event | category | flops | bytes accessed | tf_op | source)
XLA Modules:
  0.0 67.9 jit_solution(465878535600373677)
XLA Ops:
  0.6 0.0 copy-start.4
  0.6 1.2 %copy-done.4 = bf16[1,2,32,7168]{3,2,1,0:T(8,128)(2,1)S(1)} copy-done((bf16[1,2,32,7168]{3,2,1,0:T(8,128)(2,1)S(1)}, bf16[1,2,32,7168]{3,2,1,0:T(8,128)(2,1)}, u32[]{:S(2)}) %copy-start.4) | copy-done | bytes 917528
  1.8 1.6 %shard_map.95 = f32[64,1,128]{2,1,0:T(1,128)} custom-call(bf16[1,2,32,7168]{3,2,1,0:T(8,128)(2,1)S(1)} %copy-done.4), custom_call_target="tpu_custom_call" | custom-call | flops 917504 | bytes 917504 | tf_op jit(solution)/shard_map/pallas_call | solution.py:222
  3.5 12.6 %all-to-all-start = ((f32[64,1,128]{2,1,0:T(1,128)}), f32[64,1,128]{2,1,0:T(1,128)S(1)}, u32[]{:S(2)}, u32[]{:S(2)}) async-start(f32[64,1,128]{2,1,0:T(1,128)} %shard_map.95), calls=%async_computation | async-start | bytes 65536 | tf_op jit(solution)/shard_map/all_to_all | solution.py:230
  16.7 7.9 %all-to-all-done.sums = f32[64,1,128]{2,1,0:T(1,128)S(1)} async-done(((f32[64,1,128]{2,1,0:T(1,128)}), f32[64,1,128]{2,1,0:T(1,128)S(1)}, u32[]{:S(2)}, u32[]{:S(2)}) %all-to-all-start) | async-done | bytes 32800 | tf_op jit(solution)/shard_map/all_to_all | solution.py:230
  24.6 1.5 %copy-done = f32[2,32,7168]{2,1,0:T(8,128)S(1)} copy-done((f32[2,32,7168]{2,1,0:T(8,128)S(1)}, f32[2,32,7168]{2,1,0:T(8,128)}, u32[]{:S(2)}) %copy-start) | copy-done | bytes 1835032
  26.1 1.5 %copy-done.3 = f32[1,2,32,7168]{3,2,1,0:T(8,128)S(1)} copy-done((f32[1,2,32,7168]{3,2,1,0:T(8,128)S(1)}, f32[1,2,32,7168]{3,2,1,0:T(8,128)}, u32[]{:S(2)}) %copy-start.3) | copy-done | bytes 1835032
  27.6 1.2 %copy-done.5 = bf16[1,2,32,7168]{3,2,1,0:T(8,128)(2,1)S(1)} copy-done((bf16[1,2,32,7168]{3,2,1,0:T(8,128)(2,1)S(1)}, bf16[1,2,32,7168]{3,2,1,0:T(8,128)(2,1)}, u32[]{:S(2)}) %copy-start.5) | copy-done | bytes 917528
  28.8 1.2 %copy-done.7 = bf16[1,2,32,7168]{3,2,1,0:T(8,128)(2,1)S(1)} copy-done((bf16[1,2,32,7168]{3,2,1,0:T(8,128)(2,1)S(1)}, bf16[1,2,32,7168]{3,2,1,0:T(8,128)(2,1)}, u32[]{:S(2)}) %copy-start.7) | copy-done | bytes 917528
  30.0 1.2 %copy-done.8 = bf16[1,2,32,7168]{3,2,1,0:T(8,128)(2,1)S(1)} copy-done((bf16[1,2,32,7168]{3,2,1,0:T(8,128)(2,1)S(1)}, bf16[1,2,32,7168]{3,2,1,0:T(8,128)(2,1)}, u32[]{:S(2)}) %copy-start.8) | copy-done | bytes 917528
  31.2 0.7 copy-done.9
  31.8 2.3 %shard_map.98 = (bf16[16,3584]{1,0:T(8,128)(2,1)S(1)}, bf16[16,3584]{1,0:T(8,128)(2,1)S(1)}) custom-call(s32[2]{0:T(128)S(1)} %copy-done.9, s32[1]{0:T(128)S(6)} %copy.26.step, f32[64,1,128]{2,1,0:T(1,128)S(1)} %all-to-all-done.sums, f32[1,2,32,7168]{3,2,1,0:T(8,128)S(1)} %copy-done.3, bf16[1,2,32,7168]{3,2,1,0:T(8,128)(2,1)S(1)} %copy-done.7, ...), custom_call_target="tpu_custom_call" | custom-call | flops 2867200 | bytes 1835008 | tf_op jit(solution)/shard_map/pallas_call | solution.py:235
  34.1 0.0 copy-start.6
  34.1 2.2 %collective-permute-start.4 = (bf16[16,3584]{1,0:T(8,128)(2,1)S(1)}, bf16[16,3584]{1,0:T(8,128)(2,1)S(1)}, u32[]{:S(2)}, u32[]{:S(2)}) collective-permute-start(bf16[16,3584]{1,0:T(8,128)(2,1)S(1)} %get-tuple-element.17), channel_id=1, source_target_pairs={{0,64},{64,0},{128,192},{192,128},{1,65},{65,1},{129,193},{193,129... | collective-permute-start | bytes 344072 | tf_op jit(solution)/shard_map/ppermute | solution.py:209
  36.3 2.3 %shard_map.96 = (bf16[16,3584]{1,0:T(8,128)(2,1)S(1)}, bf16[16,3584]{1,0:T(8,128)(2,1)S(1)}) custom-call(s32[2]{0:T(128)S(1)} %copy-done.9, s32[1]{0:T(128)S(6)} %copy.26.step, f32[64,1,128]{2,1,0:T(1,128)S(1)} %all-to-all-done.sums, f32[1,2,32,7168]{3,2,1,0:T(8,128)S(1)} %copy-done.3, bf16[1,2,32,7168]{3,2,1,0:T(8,128)(2,1)S(1)} %copy-done.7, ...), custom_call_target="tpu_custom_call" | custom-call | flops 2867200 | bytes 1835008 | tf_op jit(solution)/shard_map/pallas_call | solution.py:235
  38.7 0.1 collective-permute-start
  38.8 0.0 collective-permute-done.4.two
  38.8 4.3 %collective-permute-start.6 = (bf16[16,3584]{1,0:T(8,128)(2,1)S(1)}, bf16[16,3584]{1,0:T(8,128)(2,1)S(1)}, u32[]{:S(2)}, u32[]{:S(2)}) collective-permute-start(bf16[16,3584]{1,0:T(8,128)(2,1)S(1)} %shard_map.99.one), channel_id=1, source_target_pairs={{0,128},{64,192},{128,0},{192,64},{1,129},{65,193},{129,1},{193,65... | collective-permute-start | bytes 344072 | tf_op jit(solution)/shard_map/ppermute | solution.py:209
  43.1 0.0 collective-permute-done.two
  43.1 0.0 copy-start.1
  43.2 1.3 %collective-permute-start.2 = (bf16[16,3584]{1,0:T(8,128)(2,1)S(1)}, bf16[16,3584]{1,0:T(8,128)(2,1)S(1)}, u32[]{:S(2)}, u32[]{:S(2)}) collective-permute-start(bf16[16,3584]{1,0:T(8,128)(2,1)S(1)} %shard_map.97.one), channel_id=1, source_target_pairs={{0,128},{64,192},{128,0},{192,64},{1,129},{65,193},{129,1},{193,65... | collective-permute-start | bytes 344072 | tf_op jit(solution)/shard_map/ppermute | solution.py:209
  44.4 1.0 %collective-permute-start.5 = (bf16[16,3584]{1,0:T(8,128)(2,1)S(1)}, bf16[16,3584]{1,0:T(8,128)(2,1)S(1)}, u32[]{:S(2)}, u32[]{:S(2)}) collective-permute-start(bf16[16,3584]{1,0:T(8,128)(2,1)S(1)} %shard_map.99.one), channel_id=1, source_target_pairs={{0,64},{64,0},{128,192},{192,128},{1,65},{65,1},{129,193},{193,129... | collective-permute-start | bytes 344072 | tf_op jit(solution)/shard_map/ppermute | solution.py:209
  45.4 1.6 %collective-permute-done.6.two = bf16[16,3584]{1,0:T(8,128)(2,1)S(1)} collective-permute-done((bf16[16,3584]{1,0:T(8,128)(2,1)S(1)}, bf16[16,3584]{1,0:T(8,128)(2,1)S(1)}, u32[]{:S(2)}, u32[]{:S(2)}) %collective-permute-start.6) | collective-permute-done | bytes 114720 | tf_op jit(solution)/shard_map/ppermute | solution.py:209
  47.0 4.5 %collective-permute-start.7 = (bf16[16,3584]{1,0:T(8,128)(2,1)S(1)}, bf16[16,3584]{1,0:T(8,128)(2,1)S(1)}, u32[]{:S(2)}, u32[]{:S(2)}) collective-permute-start(bf16[16,3584]{1,0:T(8,128)(2,1)S(1)} %collective-permute-done.6.two), channel_id=1, source_target_pairs={{0,64},{64,0},{128,192},{192,128},{1,65},{65,1},{129,193},{193,129... | collective-permute-start | bytes 344072 | tf_op jit(solution)/shard_map/ppermute | solution.py:209
  51.5 0.0 collective-permute-start.1
  51.5 3.6 %collective-permute-done.2.two = bf16[16,3584]{1,0:T(8,128)(2,1)S(1)} collective-permute-done((bf16[16,3584]{1,0:T(8,128)(2,1)S(1)}, bf16[16,3584]{1,0:T(8,128)(2,1)S(1)}, u32[]{:S(2)}, u32[]{:S(2)}) %collective-permute-start.2) | collective-permute-done | bytes 114720 | tf_op jit(solution)/shard_map/ppermute | solution.py:209
  55.1 0.7 collective-permute-start.3
  55.8 4.8 %shard_map.100 = (f32[1,2,32,7168]{3,2,1,0:T(8,128)}, f32[2,32,7168]{2,1,0:T(8,128)}) custom-call(s32[2]{0:T(128)S(1)} %copy-done.9, s32[1]{0:T(128)S(6)} %copy.26.step, f32[64,1,128]{2,1,0:T(1,128)S(1)} %all-to-all-done.sums, f32[1,2,32,7168]{3,2,1,0:T(8,128)S(1)} %copy-done.3, bf16[1,2,32,7168]{3,2,1,0:T(8,128)(2,1)S(1)} %copy-done.7, ...), custom_call_target="tpu_custom_call" | custom-call | flops 5734400 | bytes 5046272 | tf_op jit(solution)/shard_map/pallas_call | solution.py:266
  60.6 1.8 %shard_map.101 = (f32[1,2,32,7168]{3,2,1,0:T(8,128)}, f32[2,32,7168]{2,1,0:T(8,128)}) custom-call(s32[2]{0:T(128)S(1)} %copy-done.9, bf16[16,3584]{1,0:T(8,128)(2,1)S(1)} %shard_map.99.one, bf16[16,3584]{1,0:T(8,128)(2,1)S(1)} %collective-permute-done.6.two, f32[2,32,7168]{2,1,0:T(8,128)S(1)} %copy-done.1, ...), custom_call_target="tpu_custom_call", output_to_operand_aliasing={{0}: (5, {}), {1}: (6, {})} | custom-call | flops 458752 | bytes 1146880 | tf_op jit(solution)/shard_map/pallas_call | solution.py:285
  62.5 1.8 %shard_map.102 = (f32[1,2,32,7168]{3,2,1,0:T(8,128)}, f32[2,32,7168]{2,1,0:T(8,128)}) custom-call(s32[2]{0:T(128)S(1)} %copy-done.9, bf16[16,3584]{1,0:T(8,128)(2,1)S(1)} %collective-permute-done.5.one, bf16[16,3584]{1,0:T(8,128)(2,1)S(1)} %collective-permute-done.7.two, f32[2,32,7168]{2,1,0:T(8,128)S(1)} %copy-done.1, ...), custom_call_target="tpu_custom_call", output_to_operand_aliasing={{0}: (5, {}), {1}: (6, {})} | custom-call | flops 458752 | bytes 1146880 | tf_op jit(solution)/shard_map/pallas_call | solution.py:285
  64.3 1.8 %shard_map.103 = (f32[1,2,32,7168]{3,2,1,0:T(8,128)}, f32[2,32,7168]{2,1,0:T(8,128)}) custom-call(s32[2]{0:T(128)S(1)} %copy-done.9, bf16[16,3584]{1,0:T(8,128)(2,1)S(1)} %shard_map.97.one, bf16[16,3584]{1,0:T(8,128)(2,1)S(1)} %collective-permute-done.2.two, f32[2,32,7168]{2,1,0:T(8,128)S(1)} %copy-done.1, ...), custom_call_target="tpu_custom_call", output_to_operand_aliasing={{0}: (5, {}), {1}: (6, {})} | custom-call | flops 458752 | bytes 1146880 | tf_op jit(solution)/shard_map/pallas_call | solution.py:285
  66.1 1.8 %shard_map.104 = (f32[1,2,32,7168]{3,2,1,0:T(8,128)}, f32[2,32,7168]{2,1,0:T(8,128)}) custom-call(s32[2]{0:T(128)S(1)} %copy-done.9, bf16[16,3584]{1,0:T(8,128)(2,1)S(1)} %collective-permute-done.1.one, bf16[16,3584]{1,0:T(8,128)(2,1)S(1)} %collective-permute-done.3.two, f32[2,32,7168]{2,1,0:T(8,128)S(1)} %copy-done.1, ...), custom_call_target="tpu_custom_call", output_to_operand_aliasing={{0}: (5, {}), {1}: (6, {})} | custom-call | flops 458752 | bytes 1146880 | tf_op jit(solution)/shard_map/pallas_call | solution.py:285
  (16 shorter events, 0.1 us)
Async XLA Ops:
  0.6 1.2 %copy-start.4 = (bf16[1,2,32,7168]{3,2,1,0:T(8,128)(2,1)S(1)}, bf16[1,2,32,7168]{3,2,1,0:T(8,128)(2,1)}, u32[]{:S(2)}) copy-start(bf16[1,2,32,7168]{3,2,1,0:T(8,128)(2,1)} %gradient.7) | copy-start | bytes 2752516
  3.5 21.2 %all-to-all-start = ((f32[64,1,128]{2,1,0:T(1,128)}), f32[64,1,128]{2,1,0:T(1,128)S(1)}, u32[]{:S(2)}, u32[]{:S(2)}) async-start(f32[64,1,128]{2,1,0:T(1,128)} %shard_map.95), calls=%async_computation | async-start | bytes 65536 | tf_op jit(solution)/shard_map/all_to_all | solution.py:230
  24.6 1.5 %copy-start = (f32[2,32,7168]{2,1,0:T(8,128)S(1)}, f32[2,32,7168]{2,1,0:T(8,128)}, u32[]{:S(2)}) copy-start(f32[2,32,7168]{2,1,0:T(8,128)} %anchor.11) | copy-start | bytes 5505028
  26.1 1.5 %copy-start.3 = (f32[1,2,32,7168]{3,2,1,0:T(8,128)S(1)}, f32[1,2,32,7168]{3,2,1,0:T(8,128)}, u32[]{:S(2)}) copy-start(f32[1,2,32,7168]{3,2,1,0:T(8,128)} %weights.5) | copy-start | bytes 5505028
  27.6 1.2 %copy-start.5 = (bf16[1,2,32,7168]{3,2,1,0:T(8,128)(2,1)S(1)}, bf16[1,2,32,7168]{3,2,1,0:T(8,128)(2,1)}, u32[]{:S(2)}) copy-start(bf16[1,2,32,7168]{3,2,1,0:T(8,128)(2,1)} %gradient.7) | copy-start | bytes 2752516
  28.8 1.2 %copy-start.7 = (bf16[1,2,32,7168]{3,2,1,0:T(8,128)(2,1)S(1)}, bf16[1,2,32,7168]{3,2,1,0:T(8,128)(2,1)}, u32[]{:S(2)}) copy-start(bf16[1,2,32,7168]{3,2,1,0:T(8,128)(2,1)} %first.5) | copy-start | bytes 2752516
  30.0 1.2 %copy-start.8 = (bf16[1,2,32,7168]{3,2,1,0:T(8,128)(2,1)S(1)}, bf16[1,2,32,7168]{3,2,1,0:T(8,128)(2,1)}, u32[]{:S(2)}) copy-start(bf16[1,2,32,7168]{3,2,1,0:T(8,128)(2,1)} %second.5) | copy-start | bytes 2752516
  31.2 0.7 copy-start.9
  34.1 21.7 %copy-start.6 = (bf16[1,2,32,7168]{3,2,1,0:T(8,128)(2,1)S(1)}, bf16[1,2,32,7168]{3,2,1,0:T(8,128)(2,1)}, u32[]{:S(2)}) copy-start(bf16[1,2,32,7168]{3,2,1,0:T(8,128)(2,1)} %gradient.7) | copy-start | bytes 2752516
  34.1 4.6 %collective-permute-start.4 = (bf16[16,3584]{1,0:T(8,128)(2,1)S(1)}, bf16[16,3584]{1,0:T(8,128)(2,1)S(1)}, u32[]{:S(2)}, u32[]{:S(2)}) collective-permute-start(bf16[16,3584]{1,0:T(8,128)(2,1)S(1)} %get-tuple-element.17), channel_id=1, source_target_pairs={{0,64},{64,0},{128,192},{192,128},{1,65},{65,1},{129,193},{193,129... | collective-permute-start | bytes 344072 | tf_op jit(solution)/shard_map/ppermute | solution.py:209
  36.3 19.5 %copy-start.2 = (f32[2,32,7168]{2,1,0:T(8,128)S(1)}, f32[2,32,7168]{2,1,0:T(8,128)}, u32[]{:S(2)}) copy-start(f32[2,32,7168]{2,1,0:T(8,128)} %momentum.9) | copy-start | bytes 5505028
  38.7 4.5 %collective-permute-start = (bf16[16,3584]{1,0:T(8,128)(2,1)S(1)}, bf16[16,3584]{1,0:T(8,128)(2,1)S(1)}, u32[]{:S(2)}, u32[]{:S(2)}) collective-permute-start(bf16[16,3584]{1,0:T(8,128)(2,1)S(1)} %get-tuple-element.15), channel_id=1, source_target_pairs={{0,64},{64,0},{128,192},{192,128},{1,65},{65,1},{129,193},{193,129... | collective-permute-start | bytes 344072 | tf_op jit(solution)/shard_map/ppermute | solution.py:209
  38.8 8.2 %collective-permute-start.6 = (bf16[16,3584]{1,0:T(8,128)(2,1)S(1)}, bf16[16,3584]{1,0:T(8,128)(2,1)S(1)}, u32[]{:S(2)}, u32[]{:S(2)}) collective-permute-start(bf16[16,3584]{1,0:T(8,128)(2,1)S(1)} %shard_map.99.one), channel_id=1, source_target_pairs={{0,128},{64,192},{128,0},{192,64},{1,129},{65,193},{129,1},{193,65... | collective-permute-start | bytes 344072 | tf_op jit(solution)/shard_map/ppermute | solution.py:209
  43.1 17.5 %copy-start.1 = (f32[2,32,7168]{2,1,0:T(8,128)S(1)}, f32[2,32,7168]{2,1,0:T(8,128)}, u32[]{:S(2)}) copy-start(f32[2,32,7168]{2,1,0:T(8,128)} %anchor.11) | copy-start | bytes 5505028
  43.2 12.0 %collective-permute-start.2 = (bf16[16,3584]{1,0:T(8,128)(2,1)S(1)}, bf16[16,3584]{1,0:T(8,128)(2,1)S(1)}, u32[]{:S(2)}, u32[]{:S(2)}) collective-permute-start(bf16[16,3584]{1,0:T(8,128)(2,1)S(1)} %shard_map.97.one), channel_id=1, source_target_pairs={{0,128},{64,192},{128,0},{192,64},{1,129},{65,193},{129,1},{193,65... | collective-permute-start | bytes 344072 | tf_op jit(solution)/shard_map/ppermute | solution.py:209
  44.4 18.0 %collective-permute-start.5 = (bf16[16,3584]{1,0:T(8,128)(2,1)S(1)}, bf16[16,3584]{1,0:T(8,128)(2,1)S(1)}, u32[]{:S(2)}, u32[]{:S(2)}) collective-permute-start(bf16[16,3584]{1,0:T(8,128)(2,1)S(1)} %shard_map.99.one), channel_id=1, source_target_pairs={{0,64},{64,0},{128,192},{192,128},{1,65},{65,1},{129,193},{193,129... | collective-permute-start | bytes 344072 | tf_op jit(solution)/shard_map/ppermute | solution.py:209
  47.0 15.4 %collective-permute-start.7 = (bf16[16,3584]{1,0:T(8,128)(2,1)S(1)}, bf16[16,3584]{1,0:T(8,128)(2,1)S(1)}, u32[]{:S(2)}, u32[]{:S(2)}) collective-permute-start(bf16[16,3584]{1,0:T(8,128)(2,1)S(1)} %collective-permute-done.6.two), channel_id=1, source_target_pairs={{0,64},{64,0},{128,192},{192,128},{1,65},{65,1},{129,193},{193,129... | collective-permute-start | bytes 344072 | tf_op jit(solution)/shard_map/ppermute | solution.py:209
  51.5 14.5 %collective-permute-start.1 = (bf16[16,3584]{1,0:T(8,128)(2,1)S(1)}, bf16[16,3584]{1,0:T(8,128)(2,1)S(1)}, u32[]{:S(2)}, u32[]{:S(2)}) collective-permute-start(bf16[16,3584]{1,0:T(8,128)(2,1)S(1)} %shard_map.97.one), channel_id=1, source_target_pairs={{0,64},{64,0},{128,192},{192,128},{1,65},{65,1},{129,193},{193,129... | collective-permute-start | bytes 344072 | tf_op jit(solution)/shard_map/ppermute | solution.py:209
  55.1 10.9 %collective-permute-start.3 = (bf16[16,3584]{1,0:T(8,128)(2,1)S(1)}, bf16[16,3584]{1,0:T(8,128)(2,1)S(1)}, u32[]{:S(2)}, u32[]{:S(2)}) collective-permute-start(bf16[16,3584]{1,0:T(8,128)(2,1)S(1)} %collective-permute-done.2.two), channel_id=1, source_target_pairs={{0,64},{64,0},{128,192},{192,128},{1,65},{65,1},{129,193},{193,129... | collective-permute-start | bytes 344072 | tf_op jit(solution)/shard_map/ppermute | solution.py:209

commit v2 on v0

v2 whole, which is shorter than its diff:
```python
import functools
import math

import jax
import jax.numpy as jnp
from jax import lax
from jax.experimental import pallas as pl
from jax.experimental.pallas import tpu as pltpu
from jax.sharding import PartitionSpec as P

CLIP_NORM = 1.0
NORM_EPSILON = 1e-06
BETA_ONE = 0.9
BETA_TWO = 0.95
INNER_RATE = 0.03
WEIGHT_DECAY = 0.1
ADAM_EPSILON = 1e-08
OUTER_RATE = 0.7
NESTEROV = 0.9

CHUNKS = 2
STEP = 512
VMEM_LIMIT = 16 * 1024 * 1024
HIDDEN = 40_000_000

HBM = pl.BlockSpec(memory_space=pltpu.HBM)
VMEM = pl.BlockSpec(memory_space=pltpu.VMEM)
SMEM = pl.BlockSpec(memory_space=pltpu.SMEM)
F32, BF16 = jnp.float32, jnp.bfloat16


def call(kernel, out_shape, in_specs, out_specs, scratch, cost, aliases=None):
    flops, size = cost
    return pl.pallas_call(
        kernel,
        out_shape=out_shape,
        in_specs=in_specs,
        out_specs=out_specs,
        scratch_shapes=scratch,
        input_output_aliases=aliases or {},
        compiler_params=pltpu.CompilerParams(vmem_limit_bytes=VMEM_LIMIT),
        cost_estimate=pl.CostEstimate(flops=flops, bytes_accessed=size, transcendentals=0),
    )


def spread(vector, width):
    return jnp.concatenate([jnp.broadcast_to(vector, (16, 128))] * (width // 128), axis=1)


def columns_of(k):
    return pl.ds(pl.multiple_of(k * STEP, STEP), STEP)


def moment_factors(step_ref):
    step = jnp.full((1, 128), step_ref[0].astype(F32))
    first = INNER_RATE / (1.0 - jnp.exp(step * math.log(BETA_ONE)))
    second = 1.0 / (1.0 - jnp.exp(step * math.log(BETA_TWO)))
    rows = (
        BETA_ONE * first,
        (1.0 - BETA_ONE) * first,
        BETA_TWO * second,
        (1.0 - BETA_TWO) * second,
    )
    return jnp.concatenate(rows * 2, axis=0)


def adam_factors(sums_ref, factors_ref):
    square = jnp.sum(jnp.sum(sums_ref[...], axis=0), axis=1, keepdims=True)
    clip = jnp.minimum(1.0, CLIP_NORM / jnp.sqrt(jnp.broadcast_to(square, (1, 128)) + NORM_EPSILON))
    return tuple(spread(row, STEP) for row in (clip, *(factors_ref[i : i + 1] for i in range(4))))


def adam_change(first, second, gradient, factors):
    clip, a, b, c, d = factors
    scaled = gradient.astype(F32) * clip
    numerator = a * first.astype(F32) + b * scaled
    square = c * second.astype(F32) + d * (scaled * scaled)
    return numerator / (square * lax.rsqrt(square) + ADAM_EPSILON)


def squares_kernel(gradient, kept, out, sems):
    copies = []
    for i in range(2):
        copies.append(pltpu.make_async_copy(gradient.at[0, i], kept.at[i], sems.at[i]))
        copies[-1].start()
    total = jnp.zeros((32, STEP), F32)
    for i in range(2):
        copies[i].wait()

        def body(k, total, i=i):
            block = kept[i, :, columns_of(k)].astype(F32)
            return total + block * block

        total = lax.fori_loop(0, kept.shape[2] // STEP, body, total)
    row = sum(total[:, i * 128 : i * 128 + 128] for i in range(STEP // 128))
    row = jnp.sum(row, axis=0, keepdims=True)
    out[...] = jnp.broadcast_to(row[None], out.shape)


def halves():
    core = lax.rem(lax.axis_index("island"), 2)
    return pl.multiple_of((1 - core) * 16, 16), pl.multiple_of(core * 16, 16)


def prepare_kernel(
    plan, step, weights, first, second, anchor, base, firsts, seconds, factors, weight, anchors, sems
):
    fragment = plan[1]
    copies = []
    for part, row in enumerate(halves()):
        rows = pl.ds(row, 16)
        pairs = (
            (weights.at[0, fragment, rows], weight.at[part]),
            (anchor.at[fragment, rows], anchors.at[part]),
            (first.at[0, fragment, rows], firsts.at[part]),
            (second.at[0, fragment, rows], seconds.at[part]),
        )
        for i, (source, target) in enumerate(pairs):
            copies.append(pltpu.make_async_copy(source, target, sems.at[part, i]))
            copies[-1].start()
    factors[...] = moment_factors(step)
    for part in range(2):
        for copy in copies[part * 4 : part * 4 + 4]:
            copy.wait()

        def body(k, _, part=part):
            at = columns_of(k)
            decayed = (1.0 - INNER_RATE * WEIGHT_DECAY) * weight[part, :, at]
            base[part, :, at] = anchors[part, :, at] - decayed
            return 0

        lax.fori_loop(0, base.shape[2] // STEP, body, 0, unroll=True)


def pseudo_kernel(part, plan, factors, sums, base, first, second, gradient, out):
    fragment, rows = plan[1], pl.ds(halves()[part], 16)
    factors = adam_factors(sums, factors)

    def body(k, _):
        at = columns_of(k)
        change = adam_change(first[part, :, at], second[part, :, at], gradient[fragment, rows, at], factors)
        out[:, at] = (base[part, :, at] + change).astype(BF16)
        return 0

    lax.fori_loop(0, out.shape[1] // STEP, body, 0, unroll=True)


def add_kernel(one, two, out):
    out[...] = (one[...].astype(F32) + two[...].astype(F32)).astype(BF16)


def rest_kernel(
    plan, factors, sums, gradient, _, weights, first, second, anchor, momentum, weights_out, momentum_out, base, momenta, *scratch
):
    fragment = 1 - plan[1]
    buffers, (result, anchors, still, sems, out_sem) = scratch[:3], scratch[3:]
    sources = (weights, first, second)
    copies = []
    for part in range(2):
        for i, source in enumerate(sources):
            copies.append(
                pltpu.make_async_copy(
                    source.at[0, fragment, pl.ds(part * 16, 16)], buffers[i].at[part], sems.at[part, i]
                )
            )
    for part, row in enumerate(halves()):
        rows = pl.ds(row, 16)
        copies.append(pltpu.make_async_copy(anchor.at[1 - fragment, rows], anchors.at[part], sems.at[part, 3]))
        copies.append(pltpu.make_async_copy(momentum.at[1 - fragment, rows], momenta.at[part], sems.at[part, 4]))
    for copy in copies:
        copy.start()
    kept = pltpu.make_async_copy(momentum.at[fragment], still, out_sem.at[2])
    kept.start()
    factors = adam_factors(sums, factors)
    outs = []
    for part in range(2):
        for copy in copies[part * 3 : part * 3 + 3]:
            copy.wait()

        def body(k, _, part=part):
            at = columns_of(k)
            w, m, v = (buffer[part, :, at] for buffer in buffers)
            change = adam_change(m, v, gradient[fragment, pl.ds(part * 16, 16), at], factors)
            result[part, :, at] = (1.0 - INNER_RATE * WEIGHT_DECAY) * w - change
            return 0

        lax.fori_loop(0, result.shape[2] // STEP, body, 0, unroll=True)
        outs.append(
            pltpu.make_async_copy(
                result.at[part], weights_out.at[0, fragment, pl.ds(part * 16, 16)], out_sem.at[part]
            )
        )
        outs[-1].start()
    kept.wait()
    outs.append(pltpu.make_async_copy(still, momentum_out.at[fragment], out_sem.at[3]))
    outs[-1].start()
    for part in range(2):
        for copy in copies[6 + 2 * part : 8 + 2 * part]:
            copy.wait()

        def outer(k, _, part=part):
            at = columns_of(k)
            m = momenta[part, :, at]
            base[part, :, at] = anchors[part, :, at] - (OUTER_RATE * NESTEROV * NESTEROV) * m
            momenta[part, :, at] = NESTEROV * m
            return 0

        lax.fori_loop(0, result.shape[2] // STEP, outer, 0, unroll=True)
    for copy in outs:
        copy.wait()


def outer_kernel(part, plan, one, two, base, momenta, _, __, weights_out, momentum_out, weight, moment, sems):
    width = one.shape[1] // CHUNKS
    rows = pl.ds(halves()[part], 16)
    outs = []
    for j in range(CHUNKS):

        def body(k, _, j=j):
            at = pl.ds(pl.multiple_of(j * width + k * STEP, STEP), STEP)
            averaged = (one[:, at].astype(F32) + two[:, at].astype(F32)) * 0.25
            weight[:, at] = base[part, :, at] - (OUTER_RATE * (1.0 + NESTEROV)) * averaged
            moment[:, at] = momenta[part, :, at] + averaged
            return 0

        lax.fori_loop(0, width // STEP, body, 0, unroll=True)
        at = pl.ds(j * width, width)
        outs += [
            pltpu.make_async_copy(weight.at[:, at], weights_out.at[0, plan[1], rows, at], sems.at[j, 0]),
            pltpu.make_async_copy(moment.at[:, at], momentum_out.at[plan[1], rows, at], sems.at[j, 1]),
        ]
        for copy in outs[-2:]:
            copy.start()
    for copy in outs:
        copy.wait()


def swap(x, bit):
    return lax.ppermute(x, "island", [(i, i ^ bit) for i in range(lax.axis_size("island"))])


def on_device(
    local_weights, first_moment, second_moment, gradient, anchor, outer_momentum, plan, step_count
):
    local_weights, first_moment, second_moment, gradient, anchor, outer_momentum = (
        pltpu.with_memory_space_constraint(x, pltpu.HBM)
        for x in (local_weights, first_moment, second_moment, gradient, anchor, outer_momentum)
    )
    rows, columns = anchor.shape[1:]
    owners = lax.axis_size("fsdp")
    shape = jax.ShapeDtypeStruct
    dma = pltpu.SemaphoreType.DMA
    buffer = pltpu.VMEM
    two = (2, 16, columns)

    kept, squares = call(
        squares_kernel,
        [shape((2, rows, columns), BF16), shape((owners, 1, 128), F32)],
        [HBM],
        [VMEM, VMEM],
        [dma((2,))],
        (4 * rows * columns, 4 * rows * columns),
    )(gradient)
    sums = lax.all_to_all(squares, "fsdp", 0, 0)
    base, firsts, seconds, factors = call(
        prepare_kernel,
        [shape(two, F32), shape(two, BF16), shape(two, BF16), shape((8, 128), F32)],
        [SMEM, SMEM] + [HBM] * 4,
        [VMEM] * 4,
        [buffer(two, F32), buffer(two, F32), dma((2, 4))],
        (HIDDEN, HIDDEN),
    )(plan, step_count, local_weights, first_moment, second_moment, anchor)

    send, keep = (
        call(
            functools.partial(pseudo_kernel, part),
            shape((16, columns), BF16),
            [SMEM] + [VMEM] * 6,
            VMEM,
            [],
            (HIDDEN, HIDDEN) if part else (12 * rows * columns, 5 * rows * columns),
        )(plan, factors, sums, base, firsts, seconds, kept)
        for part in (0, 1)
    )
    summed = call(
        add_kernel,
        shape((16, columns), BF16),
        [VMEM, VMEM],
        VMEM,
        [],
        (16 * columns, 96 * columns),
    )(keep, swap(send, 1))
    far, theirs = swap(summed, 2), swap(summed, 1)

    *outs, outer_base, outer_momenta = call(
        rest_kernel,
        [shape(local_weights.shape, F32), shape(anchor.shape, F32), shape(two, F32), shape(two, F32)],
        [SMEM] + [VMEM] * 4 + [HBM] * 5,
        [HBM, HBM, VMEM, VMEM],
        [
            buffer(two, F32),
            buffer(two, BF16),
            buffer(two, BF16),
            buffer(two, F32),
            buffer(two, F32),
            buffer((rows, columns), F32),
            dma((2, 5)),
            dma((4,)),
        ],
        (HIDDEN, HIDDEN),
    )(plan, factors, sums, kept, summed, local_weights, first_moment, second_moment, anchor, outer_momentum)

    far, outer_base = lax.optimization_barrier((far, outer_base))
    for part, one, other in ((1, summed, far), (0, theirs, swap(far, 1))):
        outs = call(
            functools.partial(outer_kernel, part),
            [shape(local_weights.shape, F32), shape(anchor.shape, F32)],
            [SMEM] + [VMEM] * 4 + [HBM] * 2,
            [HBM, HBM],
            [buffer((16, columns), F32), buffer((16, columns), F32), dma((CHUNKS, 2))],
            (HIDDEN, HIDDEN) if part else (1, 1),
            {5: 0, 6: 1},
        )(plan, one, other, outer_base, outer_momenta, *outs)
    return tuple(outs)


def solution(mesh):
    return jax.shard_map(
        on_device,
        mesh=mesh,
        in_specs=(
            P("island", None, "fsdp", None),
            P("island", None, "fsdp", None),
            P("island", None, "fsdp", None),
            P("island", None, "fsdp", None),
            P(None, "fsdp", None),
            P(None, "fsdp", None),
            P(),
            P(),
        ),
        out_specs=(P("island", None, "fsdp", None), P(None, "fsdp", None)),
        check_vma=False,
    )
```

time: 284 us -> 48.4 us (0.17)
  blocking collectives: 165 us -> 0 us
  waiting for transfers between devices: 89.3 us -> 9.89 us
  starting transfers between devices: 0.04 us -> 23 us
  between operations: 15.4 us -> 1.35 us
  other arithmetic: 14 us -> 0 us
  Pallas kernels: 0 us -> 13.3 us
    psum x1 -> x0, blocking collectives: 165 us -> none  [on_device(): square = lax.psum(jnp.sum(gradient_f * gradient_f), 'fsdp')]
    psum x1 -> x0, waiting for transfers between devices: 89.3 us -> none  [outer_update(): lax.psum(pseudo.astype(jnp.bfloat16), 'island').astype(jnp.float32)]
    pallas_call x0 -> x8, Pallas kernels: none -> 13.3 us  [the longest x1 3.94 us: on_device(): call(rest_kernel, [shape(local_weights.shape, F32), shape(anchor.shape, F...]
    all_to_all x0 -> x1, starting transfers between devices: none -> 12.6 us  [on_device(): sums = lax.all_to_all(squares, 'fsdp', 0, 0)]
    ppermute x0 -> x4, starting transfers between devices: none -> 10.4 us  [swap(): lax.ppermute(x, 'island', [(i, i ^ bit) for i in range(lax.axis_size('isl...]
    convert_element_type x1 -> x0, other arithmetic: 6.29 us -> none  [outer_update(): pseudo.astype(jnp.bfloat16)]
    ppermute x0 -> x4, waiting for transfers between devices: none -> 4.99 us  [swap(): lax.ppermute(x, 'island', [(i, i ^ bit) for i in range(lax.axis_size('isl...]
    all_to_all x0 -> x1, waiting for transfers between devices: none -> 4.89 us  [on_device(): sums = lax.all_to_all(squares, 'fsdp', 0, 0)]
  transfers between devices with their start and end apart: 1 -> 5, of which waited for: 1 -> 3; matrix products, arithmetic and copies ran while one was open for 0% -> 0% of each run, Pallas kernels for 0% -> 18%
where the time goes in v2:
time: 48.4 us; the launch traced here: 48.2 us
  starting transfers between devices  23 us (48%)
  Pallas kernels  13.3 us (27%)
  waiting for transfers between devices  9.89 us (20%)
  between operations  1.35 us (3%)
  local copies, waits for them, and re-layouts  0.65 us (1%)
    all_to_all x1, starting transfers between devices, on_device(): sums = lax.all_to_all(squares, 'fsdp', 0, 0)  12.6 us
    ppermute x4, starting transfers between devices, swap(): lax.ppermute(x, 'island', [(i, i ^ bit) for i in range(lax.axis_size('isl...  10.4 us
    ppermute x4, waiting for transfers between devices, swap(): lax.ppermute(x, 'island', [(i, i ^ bit) for i in range(lax.axis_size('isl...  4.99 us
    all_to_all x1, waiting for transfers between devices, on_device(): sums = lax.all_to_all(squares, 'fsdp', 0, 0)  4.89 us
    pallas_call x1, Pallas kernels, on_device(): call(rest_kernel, [shape(local_weights.shape, F32), shape(anchor.shape, F...  3.94 us
    pallas_call x2, Pallas kernels, on_device(): call(functools.partial(outer_kernel, part), [shape(local_weights.shape, F...  3.09 us
    pallas_call x1, Pallas kernels, on_device(): call(prepare_kernel, [shape(two, F32), shape(two, BF16), shape(two, BF16)...  2.38 us
    pallas_call x1, Pallas kernels, on_device(): call(squares_kernel, [shape((2, rows, columns), BF16), shape((owners, 1,...  1.99 us
  transfers between devices with their start and end apart: 5, of which 3 were waited for; matrix products, arithmetic and copies ran while one was open for 0% of the time, Pallas kernels for 18%

profile of v2, /device:TPU:1, one launch (start us, length us, event | category | flops | bytes accessed | tf_op | source)
XLA Modules:
  0.0 48.2 jit_solution(11580731781629382811)
XLA Ops:
  0.6 2.0 %shard_map.96 = (bf16[2,32,7168]{2,1,0:T(8,128)(2,1)S(1)}, f32[64,1,128]{2,1,0:T(1,128)}) custom-call(bf16[1,2,32,7168]{3,2,1,0:T(8,128)(2,1)} %gradient.1), custom_call_target="tpu_custom_call" | custom-call | flops 917504 | bytes 917504 | tf_op jit(solution)/shard_map/pallas_call | solution.py:256
  2.6 12.6 %all-to-all-start = ((f32[64,1,128]{2,1,0:T(1,128)}), f32[64,1,128]{2,1,0:T(1,128)S(1)}, u32[]{:S(2)}, u32[]{:S(2)}) async-start(f32[64,1,128]{2,1,0:T(1,128)} %get-tuple-element.17), calls=%async_computation | async-start | bytes 65536 | tf_op jit(solution)/shard_map/all_to_all | solution.py:264
  15.8 0.0 copy-start
  15.9 0.6 %copy-done = s32[2]{0:T(128)S(1)} copy-done((s32[2]{0:T(128)S(1)}, s32[2]{0:T(128)}, u32[]{:S(2)}) %copy-start) | copy-done | bytes 32
  16.5 0.0 copy-start.1
  16.5 2.4 %shard_map.95 = (f32[2,16,7168]{2,1,0:T(8,128)S(1)}, bf16[2,16,7168]{2,1,0:T(8,128)(2,1)S(1)}, bf16[2,16,7168]{2,1,0:T(8,128)(2,1)S(1)}, f32[8,128]{1,0:T(8,128)S(1)}) custom-call(s32[2]{0:T(128)S(1)} %copy-done, s32[1]{0:T(128)S(6)} %copy.18.step, f32[1,2,32,7168]{3,2,1,0:T(8,128)} %weights.3, bf16[1,2,32,7168]{3,2,1,0:T(8,128)(2,1)} %first.3, ...), custom_call_target="tpu_custom_call" | custom-call | flops 40000000 | bytes 40000000 | tf_op jit(solution)/shard_map/pallas_call | solution.py:265
  18.9 4.9 %all-to-all-done.sums = f32[64,1,128]{2,1,0:T(1,128)S(1)} async-done(((f32[64,1,128]{2,1,0:T(1,128)}), f32[64,1,128]{2,1,0:T(1,128)S(1)}, u32[]{:S(2)}, u32[]{:S(2)}) %all-to-all-start) | async-done | bytes 32800 | tf_op jit(solution)/shard_map/all_to_all | solution.py:264
  23.8 0.0 copy-done.1
  23.8 0.9 %shard_map.98 = bf16[16,7168]{1,0:T(8,128)(2,1)S(1)} custom-call(s32[2]{0:T(128)S(1)} %copy-done.1, f32[8,128]{1,0:T(8,128)S(1)} %get-tuple-element.16.factors, f32[64,1,128]{2,1,0:T(1,128)S(1)} %all-to-all-done.sums, f32[2,16,7168]{2,1,0:T(8,128)S(1)} %get-tuple-element.18.base, bf16[2,16,7168]{2,1,0:T(8,128)(2,1)S(1)} %get-tuple-element.19.first, ...), custom_call_target="tpu_custom_call" | custom-call | flops 2752512 | bytes 1146880 | tf_op jit(solution)/shard_map/pallas_call | solution.py:275
  24.7 2.2 %collective-permute-start = (bf16[16,7168]{1,0:T(8,128)(2,1)S(1)}, bf16[16,7168]{1,0:T(8,128)(2,1)S(1)}, u32[]{:S(2)}, u32[]{:S(2)}) collective-permute-start(bf16[16,7168]{1,0:T(8,128)(2,1)S(1)} %shard_map.98), channel_id=1, source_target_pairs={{0,64},{64,0},{128,192},{192,128},{1,65},{65,1},{129,193},{193,129... | collective-permute-start | bytes 688136 | tf_op jit(solution)/shard_map/ppermute | solution.py:239
  26.9 0.9 %shard_map.97.one = bf16[16,7168]{1,0:T(8,128)(2,1)S(1)} custom-call(s32[2]{0:T(128)S(1)} %copy-done.1, f32[8,128]{1,0:T(8,128)S(1)} %get-tuple-element.16.factors, f32[64,1,128]{2,1,0:T(1,128)S(1)} %all-to-all-done.sums, f32[2,16,7168]{2,1,0:T(8,128)S(1)} %get-tuple-element.18.base, bf16[2,16,7168]{2,1,0:T(8,128)(2,1)S(1)} %get-tuple-element.19.first, ...), custom_call_target="tpu_custom_call" | custom-call | flops 40000000 | bytes 40000000 | tf_op jit(solution)/shard_map/pallas_call | solution.py:275
  27.9 0.2 collective-permute-done.two
  28.0 0.1 shard_map.99._.one
  28.1 4.3 %collective-permute-start.2 = (bf16[16,7168]{1,0:T(8,128)(2,1)S(1)}, bf16[16,7168]{1,0:T(8,128)(2,1)S(1)}, u32[]{:S(2)}, u32[]{:S(2)}) collective-permute-start(bf16[16,7168]{1,0:T(8,128)(2,1)S(1)} %shard_map.99._.one), channel_id=1, source_target_pairs={{0,128},{64,192},{128,0},{192,64},{1,129},{65,193},{129,1},{193,65... | collective-permute-start | bytes 688136 | tf_op jit(solution)/shard_map/ppermute | solution.py:239
  32.4 0.7 %collective-permute-start.1 = (bf16[16,7168]{1,0:T(8,128)(2,1)S(1)}, bf16[16,7168]{1,0:T(8,128)(2,1)S(1)}, u32[]{:S(2)}, u32[]{:S(2)}) collective-permute-start(bf16[16,7168]{1,0:T(8,128)(2,1)S(1)} %shard_map.99._.one), channel_id=1, source_target_pairs={{0,64},{64,0},{128,192},{192,128},{1,65},{65,1},{129,193},{193,129... | collective-permute-start | bytes 688136 | tf_op jit(solution)/shard_map/ppermute | solution.py:239
  33.1 3.9 %shard_map.100 = (f32[1,2,32,7168]{3,2,1,0:T(8,128)}, f32[2,32,7168]{2,1,0:T(8,128)}, f32[2,16,7168]{2,1,0:T(8,128)S(1)}, f32[2,16,7168]{2,1,0:T(8,128)S(1)}) custom-call(s32[2]{0:T(128)S(1)} %copy-done.1, f32[8,128]{1,0:T(8,128)S(1)} %get-tuple-element.16.factors, f32[64,1,128]{2,1,0:T(1,128)S(1)} %all-to-all-done.sums, ...), custom_call_target="tpu_custom_call" | custom-call | flops 40000000 | bytes 40000000 | tf_op jit(solution)/shard_map/pallas_call | solution.py:295
  37.0 4.8 %collective-permute-done.2.two = bf16[16,7168]{1,0:T(8,128)(2,1)S(1)} collective-permute-done((bf16[16,7168]{1,0:T(8,128)(2,1)S(1)}, bf16[16,7168]{1,0:T(8,128)(2,1)S(1)}, u32[]{:S(2)}, u32[]{:S(2)}) %collective-permute-start.2) | collective-permute-done | bytes 229408 | tf_op jit(solution)/shard_map/ppermute | solution.py:239
  41.8 3.3 %collective-permute-start.3 = (bf16[16,7168]{1,0:T(8,128)(2,1)S(1)}, bf16[16,7168]{1,0:T(8,128)(2,1)S(1)}, u32[]{:S(2)}, u32[]{:S(2)}) collective-permute-start(bf16[16,7168]{1,0:T(8,128)(2,1)S(1)} %collective-permute-done.2.two), channel_id=1, source_target_pairs={{0,64},{64,0},{128,192},{192,128},{1,65},{65,1},{129,193},{193,129... | collective-permute-start | bytes 688136 | tf_op jit(solution)/shard_map/ppermute | solution.py:239
  45.1 1.5 %shard_map.101 = (f32[1,2,32,7168]{3,2,1,0:T(8,128)}, f32[2,32,7168]{2,1,0:T(8,128)}) custom-call(s32[2]{0:T(128)S(1)} %copy-done.1, bf16[16,7168]{1,0:T(8,128)(2,1)S(1)} %shard_map.99._.one, bf16[16,7168]{1,0:T(8,128)(2,1)S(1)} %collective-permute-done.2.two, ...), custom_call_target="tpu_custom_call", output_to_operand_aliasing={{0}: (5, {}), {1}: (6, {})} | custom-call | flops 40000000 | bytes 40000000 | tf_op jit(solution)/shard_map/pallas_call | solution.py:315
  46.6 0.0 collective-permute-done.1.one
  46.6 0.0 collective-permute-done.3.two
  46.7 1.5 %shard_map.102 = (f32[1,2,32,7168]{3,2,1,0:T(8,128)}, f32[2,32,7168]{2,1,0:T(8,128)}) custom-call(s32[2]{0:T(128)S(1)} %copy-done.1, bf16[16,7168]{1,0:T(8,128)(2,1)S(1)} %collective-permute-done.1.one, bf16[16,7168]{1,0:T(8,128)(2,1)S(1)} %collective-permute-done.3.two, ...), custom_call_target="tpu_custom_call", output_to_operand_aliasing={{0}: (5, {}), {1}: (6, {})} | custom-call | flops 1 | bytes 1 | tf_op jit(solution)/shard_map/pallas_call | solution.py:315
Async XLA Ops:
  2.6 21.2 %all-to-all-start = ((f32[64,1,128]{2,1,0:T(1,128)}), f32[64,1,128]{2,1,0:T(1,128)S(1)}, u32[]{:S(2)}, u32[]{:S(2)}) async-start(f32[64,1,128]{2,1,0:T(1,128)} %get-tuple-element.17), calls=%async_computation | async-start | bytes 65536 | tf_op jit(solution)/shard_map/all_to_all | solution.py:264
  15.8 0.7 %copy-start = (s32[2]{0:T(128)S(1)}, s32[2]{0:T(128)}, u32[]{:S(2)}) copy-start(s32[2]{0:T(128)} %plan.11) | copy-start | bytes 28
  16.5 7.3 %copy-start.1 = (s32[2]{0:T(128)S(1)}, s32[2]{0:T(128)}, u32[]{:S(2)}) copy-start(s32[2]{0:T(128)} %plan.11) | copy-start | bytes 28
  24.7 3.3 %collective-permute-start = (bf16[16,7168]{1,0:T(8,128)(2,1)S(1)}, bf16[16,7168]{1,0:T(8,128)(2,1)S(1)}, u32[]{:S(2)}, u32[]{:S(2)}) collective-permute-start(bf16[16,7168]{1,0:T(8,128)(2,1)S(1)} %shard_map.98), channel_id=1, source_target_pairs={{0,64},{64,0},{128,192},{192,128},{1,65},{65,1},{129,193},{193,129... | collective-permute-start | bytes 688136 | tf_op jit(solution)/shard_map/ppermute | solution.py:239
  28.1 13.7 %collective-permute-start.2 = (bf16[16,7168]{1,0:T(8,128)(2,1)S(1)}, bf16[16,7168]{1,0:T(8,128)(2,1)S(1)}, u32[]{:S(2)}, u32[]{:S(2)}) collective-permute-start(bf16[16,7168]{1,0:T(8,128)(2,1)S(1)} %shard_map.99._.one), channel_id=1, source_target_pairs={{0,128},{64,192},{128,0},{192,64},{1,129},{65,193},{129,1},{193,65... | collective-permute-start | bytes 688136 | tf_op jit(solution)/shard_map/ppermute | solution.py:239
  32.4 14.2 %collective-permute-start.1 = (bf16[16,7168]{1,0:T(8,128)(2,1)S(1)}, bf16[16,7168]{1,0:T(8,128)(2,1)S(1)}, u32[]{:S(2)}, u32[]{:S(2)}) collective-permute-start(bf16[16,7168]{1,0:T(8,128)(2,1)S(1)} %shard_map.99._.one), channel_id=1, source_target_pairs={{0,64},{64,0},{128,192},{192,128},{1,65},{65,1},{129,193},{193,129... | collective-permute-start | bytes 688136 | tf_op jit(solution)/shard_map/ppermute | solution.py:239
  41.8 4.8 %collective-permute-start.3 = (bf16[16,7168]{1,0:T(8,128)(2,1)S(1)}, bf16[16,7168]{1,0:T(8,128)(2,1)S(1)}, u32[]{:S(2)}, u32[]{:S(2)}) collective-permute-start(bf16[16,7168]{1,0:T(8,128)(2,1)S(1)} %collective-permute-done.2.two), channel_id=1, source_target_pairs={{0,64},{64,0},{128,192},{192,128},{1,65},{65,1},{129,193},{193,129... | collective-permute-start | bytes 688136 | tf_op jit(solution)/shard_map/ppermute | solution.py:239

commit v3 on v2

--- a/solution.py
+++ b/solution.py
@@ -1,5 +1,6 @@
 import functools
 import math
+import random
 
 import jax
 import jax.numpy as jnp
@@ -18,6 +19,7 @@
 OUTER_RATE = 0.7
 NESTEROV = 0.9
 
+PIECES = 4
 CHUNKS = 2
 STEP = 512
 VMEM_LIMIT = 16 * 1024 * 1024
@@ -51,8 +53,8 @@
     return pl.ds(pl.multiple_of(k * STEP, STEP), STEP)
 
 
-def moment_factors(step_ref):
-    step = jnp.full((1, 128), step_ref[0].astype(F32))
+def factors_kernel(step, factors):
+    step = jnp.full((1, 128), step[0].astype(F32))
     first = INNER_RATE / (1.0 - jnp.exp(step * math.log(BETA_ONE)))
     second = 1.0 / (1.0 - jnp.exp(step * math.log(BETA_TWO)))
     rows = (
@@ -61,11 +63,11 @@
         BETA_TWO * second,
         (1.0 - BETA_TWO) * second,
     )
-    return jnp.concatenate(rows * 2, axis=0)
+    factors[...] = jnp.concatenate(rows * 2, axis=0)
 
 
 def adam_factors(sums_ref, factors_ref):
-    square = jnp.sum(jnp.sum(sums_ref[...], axis=0), axis=1, keepdims=True)
+    square = jnp.sum(jnp.sum(sums_ref[...], axis=0, keepdims=True), axis=1, keepdims=True)
     clip = jnp.minimum(1.0, CLIP_NORM / jnp.sqrt(jnp.broadcast_to(square, (1, 128)) + NORM_EPSILON))
     return tuple(spread(row, STEP) for row in (clip, *(factors_ref[i : i + 1] for i in range(4))))
 
@@ -78,32 +80,33 @@
     return numerator / (square * lax.rsqrt(square) + ADAM_EPSILON)
 
 
-def squares_kernel(gradient, kept, out, sems):
-    copies = []
-    for i in range(2):
-        copies.append(pltpu.make_async_copy(gradient.at[0, i], kept.at[i], sems.at[i]))
-        copies[-1].start()
-    total = jnp.zeros((32, STEP), F32)
-    for i in range(2):
-        copies[i].wait()
-
-        def body(k, total, i=i):
-            block = kept[i, :, columns_of(k)].astype(F32)
-            return total + block * block
-
-        total = lax.fori_loop(0, kept.shape[2] // STEP, body, total)
-    row = sum(total[:, i * 128 : i * 128 + 128] for i in range(STEP // 128))
-    row = jnp.sum(row, axis=0, keepdims=True)
-    out[...] = jnp.broadcast_to(row[None], out.shape)
-
-
 def halves():
     core = lax.rem(lax.axis_index("island"), 2)
     return pl.multiple_of((1 - core) * 16, 16), pl.multiple_of(core * 16, 16)
 
 
+def squares_kernel(plan, gradient, squares, chosen, whole, sems, plan_sem):
+    plan_copy = pltpu.make_async_copy(plan, chosen, plan_sem.at[0])
+    plan_copy.start()
+    width = whole.shape[2] // PIECES
+    pieces = [(i, pl.ds(j * width, width)) for i in range(2) for j in range(PIECES)]
+    copies = []
+    for n, (i, at) in enumerate(pieces):
+        copies.append(pltpu.make_async_copy(gradient.at[0, i, :, at], whole.at[i, :, at], sems.at[n]))
+        copies[-1].start()
+    total = jnp.zeros((32, 256), F32)
+    for copy, (i, at) in zip(copies, pieces, strict=True):
+        copy.wait()
+        for k in range(width // 256):
+            block = whole[i, :, pl.ds(at.start + k * 256, 256)].astype(F32)
+            total = total + block * block
+    row = jnp.sum(total[:, :128] + total[:, 128:], axis=0, keepdims=True)
+    squares[...] = jnp.broadcast_to(row, squares.shape)
+    plan_copy.wait()
+
+
 def prepare_kernel(
-    plan, step, weights, first, second, anchor, base, firsts, seconds, factors, weight, anchors, sems
+    plan, weights, first, second, gradient, anchor, base, firsts, seconds, gradients, weight, anchors, sems
 ):
     fragment = plan[1]
     copies = []
@@ -114,13 +117,13 @@
             (anchor.at[fragment, rows], anchors.at[part]),
             (first.at[0, fragment, rows], firsts.at[part]),
             (second.at[0, fragment, rows], seconds.at[part]),
+            (gradient.at[0, fragment, rows], gradients.at[part]),
         )
         for i, (source, target) in enumerate(pairs):
             copies.append(pltpu.make_async_copy(source, target, sems.at[part, i]))
             copies[-1].start()
-    factors[...] = moment_factors(step)
     for part in range(2):
-        for copy in copies[part * 4 : part * 4 + 4]:
+        for copy in copies[part * 5 : part * 5 + 5]:
             copy.wait()
 
         def body(k, _, part=part):
@@ -132,13 +135,12 @@
         lax.fori_loop(0, base.shape[2] // STEP, body, 0, unroll=True)
 
 
-def pseudo_kernel(part, plan, factors, sums, base, first, second, gradient, out):
-    fragment, rows = plan[1], pl.ds(halves()[part], 16)
+def pseudo_kernel(part, factors, sums, base, first, second, gradient, out):
     factors = adam_factors(sums, factors)
 
     def body(k, _):
         at = columns_of(k)
-        change = adam_change(first[part, :, at], second[part, :, at], gradient[fragment, rows, at], factors)
+        change = adam_change(first[part, :, at], second[part, :, at], gradient[part, :, at], factors)
         out[:, at] = (base[part, :, at] + change).astype(BF16)
         return 0
 
@@ -150,11 +152,11 @@
 
 
 def rest_kernel(
-    plan, factors, sums, gradient, _, weights, first, second, anchor, momentum, weights_out, momentum_out, base, momenta, *scratch
+    plan, factors, sums, _, gradient, weights, first, second, anchor, momentum, weights_out, momentum_out, base, momenta, *scratch
 ):
     fragment = 1 - plan[1]
-    buffers, (result, anchors, still, sems, out_sem) = scratch[:3], scratch[3:]
-    sources = (weights, first, second)
+    buffers, (result, anchors, still, sems, out_sem) = scratch[:4], scratch[4:]
+    sources = (weights, first, second, gradient)
     copies = []
     for part in range(2):
         for i, source in enumerate(sources):
@@ -165,8 +167,8 @@
             )
     for part, row in enumerate(halves()):
         rows = pl.ds(row, 16)
-        copies.append(pltpu.make_async_copy(anchor.at[1 - fragment, rows], anchors.at[part], sems.at[part, 3]))
-        copies.append(pltpu.make_async_copy(momentum.at[1 - fragment, rows], momenta.at[part], sems.at[part, 4]))
+        copies.append(pltpu.make_async_copy(anchor.at[1 - fragment, rows], anchors.at[part], sems.at[part, 4]))
+        copies.append(pltpu.make_async_copy(momentum.at[1 - fragment, rows], momenta.at[part], sems.at[part, 5]))
     for copy in copies:
         copy.start()
     kept = pltpu.make_async_copy(momentum.at[fragment], still, out_sem.at[2])
@@ -174,13 +176,13 @@
     factors = adam_factors(sums, factors)
     outs = []
     for part in range(2):
-        for copy in copies[part * 3 : part * 3 + 3]:
+        for copy in copies[part * 4 : part * 4 + 4]:
             copy.wait()
 
         def body(k, _, part=part):
             at = columns_of(k)
-            w, m, v = (buffer[part, :, at] for buffer in buffers)
-            change = adam_change(m, v, gradient[fragment, pl.ds(part * 16, 16), at], factors)
+            w, m, v, g = (buffer[part, :, at] for buffer in buffers)
+            change = adam_change(m, v, g, factors)
             result[part, :, at] = (1.0 - INNER_RATE * WEIGHT_DECAY) * w - change
             return 0
 
@@ -195,7 +197,7 @@
     outs.append(pltpu.make_async_copy(still, momentum_out.at[fragment], out_sem.at[3]))
     outs[-1].start()
     for part in range(2):
-        for copy in copies[6 + 2 * part : 8 + 2 * part]:
+        for copy in copies[8 + 2 * part : 10 + 2 * part]:
             copy.wait()
 
         def outer(k, _, part=part):
@@ -235,16 +237,30 @@
         copy.wait()
 
 
+def owner_groups():
+    def place(owner):
+        x, y, z = owner // 16, owner // 4 % 4, owner % 4
+        return z, min(x, 4 - x) + min(y, 4 - y)
+
+    owners = list(range(64))
+    random.Random(1).shuffle(owners)
+    owners.sort(key=place, reverse=True)
+    return [[island * 64 + owner for owner in owners] for island in range(4)]
+
+
 def swap(x, bit):
     return lax.ppermute(x, "island", [(i, i ^ bit) for i in range(lax.axis_size("island"))])
+
+
+def in_hbm(x):
+    return pltpu.with_memory_space_constraint(x, pltpu.HBM)
 
 
 def on_device(
     local_weights, first_moment, second_moment, gradient, anchor, outer_momentum, plan, step_count
 ):
     local_weights, first_moment, second_moment, gradient, anchor, outer_momentum = (
-        pltpu.with_memory_space_constraint(x, pltpu.HBM)
-        for x in (local_weights, first_moment, second_moment, gradient, anchor, outer_momentum)
+        in_hbm(x) for x in (local_weights, first_moment, second_moment, gradient, anchor, outer_momentum)
     )
     rows, columns = anchor.shape[1:]
     owners = lax.axis_size("fsdp")
@@ -253,33 +269,36 @@
     buffer = pltpu.VMEM
     two = (2, 16, columns)
 
-    kept, squares = call(
+    squares, chosen = call(
         squares_kernel,
-        [shape((2, rows, columns), BF16), shape((owners, 1, 128), F32)],
-        [HBM],
-        [VMEM, VMEM],
-        [dma((2,))],
+        [shape((owners, 128), F32), pltpu.SMEM((2,), jnp.int32)],
+        [HBM] * 2,
+        [VMEM, SMEM],
+        [buffer((2, rows, columns), BF16), dma((2 * PIECES,)), dma((1,))],
         (4 * rows * columns, 4 * rows * columns),
-    )(gradient)
-    sums = lax.all_to_all(squares, "fsdp", 0, 0)
-    base, firsts, seconds, factors = call(
+    )(in_hbm(plan), gradient)
+    step_count, squares = lax.optimization_barrier((step_count, squares))
+    sums = lax.all_to_all(
+        squares.reshape(owners, 1, 128), ("island", "fsdp"), 0, 0, axis_index_groups=owner_groups()
+    ).reshape(owners, 128)
+    base, firsts, seconds, gradients = call(
         prepare_kernel,
-        [shape(two, F32), shape(two, BF16), shape(two, BF16), shape((8, 128), F32)],
-        [SMEM, SMEM] + [HBM] * 4,
+        [shape(two, F32)] + [shape(two, BF16)] * 3,
+        [SMEM] + [HBM] * 5,
         [VMEM] * 4,
-        [buffer(two, F32), buffer(two, F32), dma((2, 4))],
+        [buffer(two, F32), buffer(two, F32), dma((2, 5))],
         (HIDDEN, HIDDEN),
-    )(plan, step_count, local_weights, first_moment, second_moment, anchor)
-
+    )(chosen, local_weights, first_moment, second_moment, gradient, anchor)
+    factors = call(factors_kernel, shape((8, 128), F32), [SMEM], VMEM, [], (HIDDEN, HIDDEN))(step_count)
     send, keep = (
         call(
             functools.partial(pseudo_kernel, part),
             shape((16, columns), BF16),
-            [SMEM] + [VMEM] * 6,
+            [VMEM] * 6,
             VMEM,
             [],
             (HIDDEN, HIDDEN) if part else (12 * rows * columns, 5 * rows * columns),
-        )(plan, factors, sums, base, firsts, seconds, kept)
+        )(factors, sums, base, firsts, seconds, gradients)
         for part in (0, 1)
     )
     summed = call(
@@ -295,20 +314,21 @@
     *outs, outer_base, outer_momenta = call(
         rest_kernel,
         [shape(local_weights.shape, F32), shape(anchor.shape, F32), shape(two, F32), shape(two, F32)],
-        [SMEM] + [VMEM] * 4 + [HBM] * 5,
+        [SMEM] + [VMEM] * 3 + [HBM] * 6,
         [HBM, HBM, VMEM, VMEM],
         [
             buffer(two, F32),
             buffer(two, BF16),
             buffer(two, BF16),
+            buffer(two, BF16),
             buffer(two, F32),
             buffer(two, F32),
             buffer((rows, columns), F32),
-            dma((2, 5)),
+            dma((2, 6)),
             dma((4,)),
         ],
         (HIDDEN, HIDDEN),
-    )(plan, factors, sums, kept, summed, local_weights, first_moment, second_moment, anchor, outer_momentum)
+    )(chosen, factors, sums, summed, gradient, local_weights, first_moment, second_moment, anchor, outer_momentum)
 
     far, outer_base = lax.optimization_barrier((far, outer_base))
     for part, one, other in ((1, summed, far), (0, theirs, swap(far, 1))):
@@ -320,7 +340,7 @@
             [buffer((16, columns), F32), buffer((16, columns), F32), dma((CHUNKS, 2))],
             (HIDDEN, HIDDEN) if part else (1, 1),
             {5: 0, 6: 1},
-        )(plan, one, other, outer_base, outer_momenta, *outs)
+        )(chosen, one, other, outer_base, outer_momenta, *outs)
     return tuple(outs)
 
 

time: 48.4 us -> 40.1 us (0.83)
  the two profiles are of different devices: /device:TPU:1 before, /device:TPU:33 now
where the time goes in v3:
time: 40.1 us; the launch traced here: 39.9 us
  starting transfers between devices  21.1 us (53%)
  Pallas kernels  10.3 us (26%)
  waiting for transfers between devices  7.13 us (18%)
  between operations  1.35 us (3%)
    all_to_all x1, starting transfers between devices, on_device(): lax.all_to_all(squares.reshape(owners, 1, 128), ('island', 'fsdp'), 0, 0,...  12.4 us
    ppermute x4, starting transfers between devices, swap(): lax.ppermute(x, 'island', [(i, i ^ bit) for i in range(lax.axis_size('isl...  8.7 us
    ppermute x4, waiting for transfers between devices, swap(): lax.ppermute(x, 'island', [(i, i ^ bit) for i in range(lax.axis_size('isl...  7.12 us
    pallas_call x1, Pallas kernels, on_device(): call(rest_kernel, [shape(local_weights.shape, F32), shape(anchor.shape, F...  3.56 us
    pallas_call x2, Pallas kernels, on_device(): call(functools.partial(outer_kernel, part), [shape(local_weights.shape, F...  2 us
    pallas_call x1, Pallas kernels, on_device(): call(prepare_kernel, [shape(two, F32)] + [shape(two, BF16)] * 3, [SMEM] +...  2 us
    pallas_call x1, Pallas kernels, on_device(): call(squares_kernel, [shape((owners, 128), F32), pltpu.SMEM((2,), jnp.int...  1.98 us
  transfers between devices with their start and end apart: 5, of which 3 were waited for; matrix products, arithmetic and copies ran while one was open for 0% of the time, Pallas kernels for 17%

profile of v3, /device:TPU:33, one launch (start us, length us, event | category | flops | bytes accessed | tf_op | source)
XLA Modules:
  0.0 39.9 jit_solution(7400739282064046082)
XLA Ops:
  0.6 2.0 %shard_map.95 = (f32[64,128]{1,0:T(8,128)}, s32[2]{0:T(128)S(4)}) custom-call(s32[2]{0:T(128)} %plan.1, bf16[1,2,32,7168]{3,2,1,0:T(8,128)(2,1)} %gradient.5), custom_call_target="tpu_custom_call" | custom-call | flops 917504 | bytes 917504 | tf_op jit(solution)/shard_map/pallas_call | solution.py:272
  2.6 12.4 %all-to-all-start = ((f32[64,1,128]{2,1,0:T(1,128)}), f32[64,1,128]{2,1,0:T(1,128)S(1)}, u32[]{:S(2)}, u32[]{:S(2)}) async-start(f32[64,1,128]{2,1,0:T(1,128)} %bitcast.1), calls=%async_computation | async-start | bytes 65536 | tf_op jit(solution)/shard_map/all_to_all | solution.py:281
  15.7 2.0 %shard_map.97 = (f32[2,16,7168]{2,1,0:T(8,128)S(1)}, bf16[2,16,7168]{2,1,0:T(8,128)(2,1)S(1)}, bf16[2,16,7168]{2,1,0:T(8,128)(2,1)S(1)}, bf16[2,16,7168]{2,1,0:T(8,128)(2,1)S(1)}) custom-call(s32[2]{0:T(128)S(4)} %get-tuple-element.18.plan, f32[1,2,32,7168]{3,2,1,0:T(8,128)} %weights.3, bf16[1,2,32,7168]{3,2,1,0:T(8,128)(2,1)} %first.3, ...), custom_call_target="tpu_custom_call" | custom-call | flops 40000000 | bytes 40000000 | tf_op jit(solution)/shard_map/pallas_call | solution.py:284
  17.7 0.0 all-to-all-done
  17.7 0.3 shard_map.99
  18.1 1.5 %collective-permute-start = (bf16[16,7168]{1,0:T(8,128)(2,1)S(1)}, bf16[16,7168]{1,0:T(8,128)(2,1)S(1)}, u32[]{:S(2)}, u32[]{:S(2)}) collective-permute-start(bf16[16,7168]{1,0:T(8,128)(2,1)S(1)} %shard_map.99), channel_id=1, source_target_pairs={{0,64},{64,0},{128,192},{192,128},{1,65},{65,1},{129,193},{193,129... | collective-permute-start | bytes 688136 | tf_op jit(solution)/shard_map/ppermute | solution.py:252
  19.6 0.3 shard_map.98.one
  19.9 0.8 %collective-permute-done.two = bf16[16,7168]{1,0:T(8,128)(2,1)S(1)} collective-permute-done((bf16[16,7168]{1,0:T(8,128)(2,1)S(1)}, bf16[16,7168]{1,0:T(8,128)(2,1)S(1)}, u32[]{:S(2)}, u32[]{:S(2)}) %collective-permute-start) | collective-permute-done | bytes 229408 | tf_op jit(solution)/shard_map/ppermute | solution.py:252
  20.7 0.1 shard_map.100._.one
  20.8 5.2 %collective-permute-start.2 = (bf16[16,7168]{1,0:T(8,128)(2,1)S(1)}, bf16[16,7168]{1,0:T(8,128)(2,1)S(1)}, u32[]{:S(2)}, u32[]{:S(2)}) collective-permute-start(bf16[16,7168]{1,0:T(8,128)(2,1)S(1)} %shard_map.100._.one), channel_id=1, source_target_pairs={{0,128},{64,192},{128,0},{192,64},{1,129},{65,193},{129,1},{193,65... | collective-permute-start | bytes 688136 | tf_op jit(solution)/shard_map/ppermute | solution.py:252
  26.0 0.7 %collective-permute-start.1 = (bf16[16,7168]{1,0:T(8,128)(2,1)S(1)}, bf16[16,7168]{1,0:T(8,128)(2,1)S(1)}, u32[]{:S(2)}, u32[]{:S(2)}) collective-permute-start(bf16[16,7168]{1,0:T(8,128)(2,1)S(1)} %shard_map.100._.one), channel_id=1, source_target_pairs={{0,64},{64,0},{128,192},{192,128},{1,65},{65,1},{129,193},{193,129... | collective-permute-start | bytes 688136 | tf_op jit(solution)/shard_map/ppermute | solution.py:252
  26.7 3.6 %shard_map.101 = (f32[1,2,32,7168]{3,2,1,0:T(8,128)}, f32[2,32,7168]{2,1,0:T(8,128)}, f32[2,16,7168]{2,1,0:T(8,128)S(1)}, f32[2,16,7168]{2,1,0:T(8,128)S(1)}) custom-call(s32[2]{0:T(128)S(4)} %get-tuple-element.18.plan, f32[8,128]{1,0:T(8,128)S(1)} %shard_map.96.factors, f32[64,128]{1,0:T(8,128)S(1)} %bitcast.6, bf16[16,7168]{1,0:T(8,128)(2,1)S(1)} %shard_map.100._.one, ...), custom_call_target="tpu_custom_call" | custom-call | flops 40000000 | bytes 40000000 | tf_op jit(solution)/shard_map/pallas_call | solution.py:314
  30.2 6.3 %collective-permute-done.2.two = bf16[16,7168]{1,0:T(8,128)(2,1)S(1)} collective-permute-done((bf16[16,7168]{1,0:T(8,128)(2,1)S(1)}, bf16[16,7168]{1,0:T(8,128)(2,1)S(1)}, u32[]{:S(2)}, u32[]{:S(2)}) %collective-permute-start.2) | collective-permute-done | bytes 229408 | tf_op jit(solution)/shard_map/ppermute | solution.py:252
  36.5 1.3 %collective-permute-start.3 = (bf16[16,7168]{1,0:T(8,128)(2,1)S(1)}, bf16[16,7168]{1,0:T(8,128)(2,1)S(1)}, u32[]{:S(2)}, u32[]{:S(2)}) collective-permute-start(bf16[16,7168]{1,0:T(8,128)(2,1)S(1)} %collective-permute-done.2.two), channel_id=1, source_target_pairs={{0,64},{64,0},{128,192},{192,128},{1,65},{65,1},{129,193},{193,129... | collective-permute-start | bytes 688136 | tf_op jit(solution)/shard_map/ppermute | solution.py:252
  37.8 1.0 %shard_map.102 = (f32[1,2,32,7168]{3,2,1,0:T(8,128)}, f32[2,32,7168]{2,1,0:T(8,128)}) custom-call(s32[2]{0:T(128)S(4)} %get-tuple-element.18.plan, bf16[16,7168]{1,0:T(8,128)(2,1)S(1)} %shard_map.100._.one, bf16[16,7168]{1,0:T(8,128)(2,1)S(1)} %collective-permute-done.2.two, ...), custom_call_target="tpu_custom_call", output_to_operand_aliasing={{0}: (5, {}), {1}: (6, {})} | custom-call | flops 40000000 | bytes 40000000 | tf_op jit(solution)/shard_map/pallas_call | solution.py:335
  38.8 0.0 collective-permute-done.1.one
  38.8 0.1 collective-permute-done.3.two
  38.9 1.0 %shard_map.103 = (f32[1,2,32,7168]{3,2,1,0:T(8,128)}, f32[2,32,7168]{2,1,0:T(8,128)}) custom-call(s32[2]{0:T(128)S(4)} %get-tuple-element.18.plan, bf16[16,7168]{1,0:T(8,128)(2,1)S(1)} %collective-permute-done.1.one, bf16[16,7168]{1,0:T(8,128)(2,1)S(1)} %collective-permute-done.3.two, ...), custom_call_target="tpu_custom_call", output_to_operand_aliasing={{0}: (5, {}), {1}: (6, {})} | custom-call | flops 1 | bytes 1 | tf_op jit(solution)/shard_map/pallas_call | solution.py:335
  (1 shorter events, 0.0 us)
Async XLA Ops:
  2.6 15.1 %all-to-all-start = ((f32[64,1,128]{2,1,0:T(1,128)}), f32[64,1,128]{2,1,0:T(1,128)S(1)}, u32[]{:S(2)}, u32[]{:S(2)}) async-start(f32[64,1,128]{2,1,0:T(1,128)} %bitcast.1), calls=%async_computation | async-start | bytes 65536 | tf_op jit(solution)/shard_map/all_to_all | solution.py:281
  18.1 2.6 %collective-permute-start = (bf16[16,7168]{1,0:T(8,128)(2,1)S(1)}, bf16[16,7168]{1,0:T(8,128)(2,1)S(1)}, u32[]{:S(2)}, u32[]{:S(2)}) collective-permute-start(bf16[16,7168]{1,0:T(8,128)(2,1)S(1)} %shard_map.99), channel_id=1, source_target_pairs={{0,64},{64,0},{128,192},{192,128},{1,65},{65,1},{129,193},{193,129... | collective-permute-start | bytes 688136 | tf_op jit(solution)/shard_map/ppermute | solution.py:252
  20.8 15.7 %collective-permute-start.2 = (bf16[16,7168]{1,0:T(8,128)(2,1)S(1)}, bf16[16,7168]{1,0:T(8,128)(2,1)S(1)}, u32[]{:S(2)}, u32[]{:S(2)}) collective-permute-start(bf16[16,7168]{1,0:T(8,128)(2,1)S(1)} %shard_map.100._.one), channel_id=1, source_target_pairs={{0,128},{64,192},{128,0},{192,64},{1,129},{65,193},{129,1},{193,65... | collective-permute-start | bytes 688136 | tf_op jit(solution)/shard_map/ppermute | solution.py:252
  26.0 12.8 %collective-permute-start.1 = (bf16[16,7168]{1,0:T(8,128)(2,1)S(1)}, bf16[16,7168]{1,0:T(8,128)(2,1)S(1)}, u32[]{:S(2)}, u32[]{:S(2)}) collective-permute-start(bf16[16,7168]{1,0:T(8,128)(2,1)S(1)} %shard_map.100._.one), channel_id=1, source_target_pairs={{0,64},{64,0},{128,192},{192,128},{1,65},{65,1},{129,193},{193,129... | collective-permute-start | bytes 688136 | tf_op jit(solution)/shard_map/ppermute | solution.py:252
  36.5 2.4 %collective-permute-start.3 = (bf16[16,7168]{1,0:T(8,128)(2,1)S(1)}, bf16[16,7168]{1,0:T(8,128)(2,1)S(1)}, u32[]{:S(2)}, u32[]{:S(2)}) collective-permute-start(bf16[16,7168]{1,0:T(8,128)(2,1)S(1)} %collective-permute-done.2.two), channel_id=1, source_target_pairs={{0,64},{64,0},{128,192},{192,128},{1,65},{65,1},{129,193},{193,129... | collective-permute-start | bytes 688136 | tf_op jit(solution)/shard_map/ppermute | solution.py:252

commit v4 on v3

--- a/solution.py
+++ b/solution.py
@@ -238,14 +238,18 @@
 
 
 def owner_groups():
-    def place(owner):
-        x, y, z = owner // 16, owner // 4 % 4, owner % 4
-        return z, min(x, 4 - x) + min(y, 4 - y)
-
     owners = list(range(64))
     random.Random(1).shuffle(owners)
-    owners.sort(key=place, reverse=True)
-    return [[island * 64 + owner for owner in owners] for island in range(4)]
+
+    def order(planes):
+        def place(owner):
+            x, y, z = owner // 16, owner // 4 % 4, owner % 4
+            return planes.index(z), -min(x, 4 - x) - min(y, 4 - y)
+
+        return sorted(owners, key=place)
+
+    orders = (order((2, 0, 3, 1)), order((3, 0, 2, 1)))
+    return [[island * 64 + owner for owner in orders[island % 2]] for island in range(4)]
 
 
 def swap(x, bit):

time: 40.1 us -> 39.6 us (0.988)
  starting transfers between devices: 21.1 us -> 20.1 us
  waiting for transfers between devices: 7.13 us -> 7.64 us
    ppermute x4, starting transfers between devices: 8.7 us -> 7.6 us  [swap(): lax.ppermute(x, 'island', [(i, i ^ bit) for i in range(lax.axis_size('isl...]
    ppermute x4, waiting for transfers between devices: 7.12 us -> 7.63 us  [swap(): lax.ppermute(x, 'island', [(i, i ^ bit) for i in range(lax.axis_size('isl...]
  transfers between devices with their start and end apart: 5 -> 5, of which waited for: 3 -> 3; matrix products, arithmetic and copies ran while one was open for 0% -> 0% of each run, Pallas kernels for 17% -> 18%
where the time goes in v4:
time: 39.6 us; the launch traced here: 39.4 us
  starting transfers between devices  20.1 us (51%)
  Pallas kernels  10.3 us (26%)
  waiting for transfers between devices  7.64 us (19%)
  between operations  1.35 us (3%)
    all_to_all x1, starting transfers between devices, on_device(): lax.all_to_all(squares.reshape(owners, 1, 128), ('island', 'fsdp'), 0, 0,...  12.5 us
    ppermute x4, waiting for transfers between devices, swap(): lax.ppermute(x, 'island', [(i, i ^ bit) for i in range(lax.axis_size('isl...  7.63 us
    ppermute x4, starting transfers between devices, swap(): lax.ppermute(x, 'island', [(i, i ^ bit) for i in range(lax.axis_size('isl...  7.6 us
    pallas_call x1, Pallas kernels, on_device(): call(rest_kernel, [shape(local_weights.shape, F32), shape(anchor.shape, F...  3.56 us
    pallas_call x2, Pallas kernels, on_device(): call(functools.partial(outer_kernel, part), [shape(local_weights.shape, F...  2 us
    pallas_call x1, Pallas kernels, on_device(): call(prepare_kernel, [shape(two, F32)] + [shape(two, BF16)] * 3, [SMEM] +...  2 us
    pallas_call x1, Pallas kernels, on_device(): call(squares_kernel, [shape((owners, 128), F32), pltpu.SMEM((2,), jnp.int...  1.98 us
  transfers between devices with their start and end apart: 5, of which 3 were waited for; matrix products, arithmetic and copies ran while one was open for 0% of the time, Pallas kernels for 18%

profile of v4, /device:TPU:33, one launch (start us, length us, event | category | flops | bytes accessed | tf_op | source)
XLA Modules:
  0.0 39.4 jit_solution(7290063945187903005)
XLA Ops:
  0.6 2.0 %shard_map.95 = (f32[64,128]{1,0:T(8,128)}, s32[2]{0:T(128)S(4)}) custom-call(s32[2]{0:T(128)} %plan.1, bf16[1,2,32,7168]{3,2,1,0:T(8,128)(2,1)} %gradient.5), custom_call_target="tpu_custom_call" | custom-call | flops 917504 | bytes 917504 | tf_op jit(solution)/shard_map/pallas_call | solution.py:276
  2.6 12.5 %all-to-all-start = ((f32[64,1,128]{2,1,0:T(1,128)}), f32[64,1,128]{2,1,0:T(1,128)S(1)}, u32[]{:S(2)}, u32[]{:S(2)}) async-start(f32[64,1,128]{2,1,0:T(1,128)} %bitcast.1), calls=%async_computation | async-start | bytes 65536 | tf_op jit(solution)/shard_map/all_to_all | solution.py:285
  15.8 2.0 %shard_map.97 = (f32[2,16,7168]{2,1,0:T(8,128)S(1)}, bf16[2,16,7168]{2,1,0:T(8,128)(2,1)S(1)}, bf16[2,16,7168]{2,1,0:T(8,128)(2,1)S(1)}, bf16[2,16,7168]{2,1,0:T(8,128)(2,1)S(1)}) custom-call(s32[2]{0:T(128)S(4)} %get-tuple-element.18.plan, f32[1,2,32,7168]{3,2,1,0:T(8,128)} %weights.3, bf16[1,2,32,7168]{3,2,1,0:T(8,128)(2,1)} %first.3, ...), custom_call_target="tpu_custom_call" | custom-call | flops 40000000 | bytes 40000000 | tf_op jit(solution)/shard_map/pallas_call | solution.py:288
  17.8 0.0 all-to-all-done
  17.9 0.3 shard_map.99
  18.2 0.9 %collective-permute-start = (bf16[16,7168]{1,0:T(8,128)(2,1)S(1)}, bf16[16,7168]{1,0:T(8,128)(2,1)S(1)}, u32[]{:S(2)}, u32[]{:S(2)}) collective-permute-start(bf16[16,7168]{1,0:T(8,128)(2,1)S(1)} %shard_map.99), channel_id=1, source_target_pairs={{0,64},{64,0},{128,192},{192,128},{1,65},{65,1},{129,193},{193,129... | collective-permute-start | bytes 688136 | tf_op jit(solution)/shard_map/ppermute | solution.py:256
  19.1 0.3 shard_map.98.one
  19.5 0.8 %collective-permute-done.two = bf16[16,7168]{1,0:T(8,128)(2,1)S(1)} collective-permute-done((bf16[16,7168]{1,0:T(8,128)(2,1)S(1)}, bf16[16,7168]{1,0:T(8,128)(2,1)S(1)}, u32[]{:S(2)}, u32[]{:S(2)}) %collective-permute-start) | collective-permute-done | bytes 229408 | tf_op jit(solution)/shard_map/ppermute | solution.py:256
  20.2 0.1 shard_map.100._.one
  20.3 4.7 %collective-permute-start.2 = (bf16[16,7168]{1,0:T(8,128)(2,1)S(1)}, bf16[16,7168]{1,0:T(8,128)(2,1)S(1)}, u32[]{:S(2)}, u32[]{:S(2)}) collective-permute-start(bf16[16,7168]{1,0:T(8,128)(2,1)S(1)} %shard_map.100._.one), channel_id=1, source_target_pairs={{0,128},{64,192},{128,0},{192,64},{1,129},{65,193},{129,1},{193,65... | collective-permute-start | bytes 688136 | tf_op jit(solution)/shard_map/ppermute | solution.py:256
  25.0 0.7 %collective-permute-start.1 = (bf16[16,7168]{1,0:T(8,128)(2,1)S(1)}, bf16[16,7168]{1,0:T(8,128)(2,1)S(1)}, u32[]{:S(2)}, u32[]{:S(2)}) collective-permute-start(bf16[16,7168]{1,0:T(8,128)(2,1)S(1)} %shard_map.100._.one), channel_id=1, source_target_pairs={{0,64},{64,0},{128,192},{192,128},{1,65},{65,1},{129,193},{193,129... | collective-permute-start | bytes 688136 | tf_op jit(solution)/shard_map/ppermute | solution.py:256
  25.7 3.6 %shard_map.101 = (f32[1,2,32,7168]{3,2,1,0:T(8,128)}, f32[2,32,7168]{2,1,0:T(8,128)}, f32[2,16,7168]{2,1,0:T(8,128)S(1)}, f32[2,16,7168]{2,1,0:T(8,128)S(1)}) custom-call(s32[2]{0:T(128)S(4)} %get-tuple-element.18.plan, f32[8,128]{1,0:T(8,128)S(1)} %shard_map.96.factors, f32[64,128]{1,0:T(8,128)S(1)} %bitcast.6, bf16[16,7168]{1,0:T(8,128)(2,1)S(1)} %shard_map.100._.one, ...), custom_call_target="tpu_custom_call" | custom-call | flops 40000000 | bytes 40000000 | tf_op jit(solution)/shard_map/pallas_call | solution.py:318
  29.3 6.8 %collective-permute-done.2.two = bf16[16,7168]{1,0:T(8,128)(2,1)S(1)} collective-permute-done((bf16[16,7168]{1,0:T(8,128)(2,1)S(1)}, bf16[16,7168]{1,0:T(8,128)(2,1)S(1)}, u32[]{:S(2)}, u32[]{:S(2)}) %collective-permute-start.2) | collective-permute-done | bytes 229408 | tf_op jit(solution)/shard_map/ppermute | solution.py:256
  36.0 1.3 %collective-permute-start.3 = (bf16[16,7168]{1,0:T(8,128)(2,1)S(1)}, bf16[16,7168]{1,0:T(8,128)(2,1)S(1)}, u32[]{:S(2)}, u32[]{:S(2)}) collective-permute-start(bf16[16,7168]{1,0:T(8,128)(2,1)S(1)} %collective-permute-done.2.two), channel_id=1, source_target_pairs={{0,64},{64,0},{128,192},{192,128},{1,65},{65,1},{129,193},{193,129... | collective-permute-start | bytes 688136 | tf_op jit(solution)/shard_map/ppermute | solution.py:256
  37.3 1.0 %shard_map.102 = (f32[1,2,32,7168]{3,2,1,0:T(8,128)}, f32[2,32,7168]{2,1,0:T(8,128)}) custom-call(s32[2]{0:T(128)S(4)} %get-tuple-element.18.plan, bf16[16,7168]{1,0:T(8,128)(2,1)S(1)} %shard_map.100._.one, bf16[16,7168]{1,0:T(8,128)(2,1)S(1)} %collective-permute-done.2.two, ...), custom_call_target="tpu_custom_call", output_to_operand_aliasing={{0}: (5, {}), {1}: (6, {})} | custom-call | flops 40000000 | bytes 40000000 | tf_op jit(solution)/shard_map/pallas_call | solution.py:339
  38.3 0.0 collective-permute-done.1.one
  38.3 0.1 collective-permute-done.3.two
  38.4 1.0 %shard_map.103 = (f32[1,2,32,7168]{3,2,1,0:T(8,128)}, f32[2,32,7168]{2,1,0:T(8,128)}) custom-call(s32[2]{0:T(128)S(4)} %get-tuple-element.18.plan, bf16[16,7168]{1,0:T(8,128)(2,1)S(1)} %collective-permute-done.1.one, bf16[16,7168]{1,0:T(8,128)(2,1)S(1)} %collective-permute-done.3.two, ...), custom_call_target="tpu_custom_call", output_to_operand_aliasing={{0}: (5, {}), {1}: (6, {})} | custom-call | flops 1 | bytes 1 | tf_op jit(solution)/shard_map/pallas_call | solution.py:339
  (1 shorter events, 0.0 us)
Async XLA Ops:
  2.6 15.2 %all-to-all-start = ((f32[64,1,128]{2,1,0:T(1,128)}), f32[64,1,128]{2,1,0:T(1,128)S(1)}, u32[]{:S(2)}, u32[]{:S(2)}) async-start(f32[64,1,128]{2,1,0:T(1,128)} %bitcast.1), calls=%async_computation | async-start | bytes 65536 | tf_op jit(solution)/shard_map/all_to_all | solution.py:285
  18.2 2.0 %collective-permute-start = (bf16[16,7168]{1,0:T(8,128)(2,1)S(1)}, bf16[16,7168]{1,0:T(8,128)(2,1)S(1)}, u32[]{:S(2)}, u32[]{:S(2)}) collective-permute-start(bf16[16,7168]{1,0:T(8,128)(2,1)S(1)} %shard_map.99), channel_id=1, source_target_pairs={{0,64},{64,0},{128,192},{192,128},{1,65},{65,1},{129,193},{193,129... | collective-permute-start | bytes 688136 | tf_op jit(solution)/shard_map/ppermute | solution.py:256
  20.3 15.7 %collective-permute-start.2 = (bf16[16,7168]{1,0:T(8,128)(2,1)S(1)}, bf16[16,7168]{1,0:T(8,128)(2,1)S(1)}, u32[]{:S(2)}, u32[]{:S(2)}) collective-permute-start(bf16[16,7168]{1,0:T(8,128)(2,1)S(1)} %shard_map.100._.one), channel_id=1, source_target_pairs={{0,128},{64,192},{128,0},{192,64},{1,129},{65,193},{129,1},{193,65... | collective-permute-start | bytes 688136 | tf_op jit(solution)/shard_map/ppermute | solution.py:256
  25.0 13.3 %collective-permute-start.1 = (bf16[16,7168]{1,0:T(8,128)(2,1)S(1)}, bf16[16,7168]{1,0:T(8,128)(2,1)S(1)}, u32[]{:S(2)}, u32[]{:S(2)}) collective-permute-start(bf16[16,7168]{1,0:T(8,128)(2,1)S(1)} %shard_map.100._.one), channel_id=1, source_target_pairs={{0,64},{64,0},{128,192},{192,128},{1,65},{65,1},{129,193},{193,129... | collective-permute-start | bytes 688136 | tf_op jit(solution)/shard_map/ppermute | solution.py:256
  36.0 2.4 %collective-permute-start.3 = (bf16[16,7168]{1,0:T(8,128)(2,1)S(1)}, bf16[16,7168]{1,0:T(8,128)(2,1)S(1)}, u32[]{:S(2)}, u32[]{:S(2)}) collective-permute-start(bf16[16,7168]{1,0:T(8,128)(2,1)S(1)} %collective-permute-done.2.two), channel_id=1, source_target_pairs={{0,64},{64,0},{128,192},{192,128},{1,65},{65,1},{129,193},{193,129... | collective-permute-start | bytes 688136 | tf_op jit(solution)/shard_map/ppermute | solution.py:256

commit v5 on v4

--- a/solution.py
+++ b/solution.py
@@ -20,6 +20,7 @@
 NESTEROV = 0.9
 
 PIECES = 4
+BEFORE = 512
 CHUNKS = 2
 STEP = 512
 VMEM_LIMIT = 16 * 1024 * 1024
@@ -147,58 +148,71 @@
     lax.fori_loop(0, out.shape[1] // STEP, body, 0, unroll=True)
 
 
-def add_kernel(one, two, out):
+def add_kernel(one, two, _, out):
     out[...] = (one[...].astype(F32) + two[...].astype(F32)).astype(BF16)
 
 
-def rest_kernel(
-    plan, factors, sums, _, gradient, weights, first, second, anchor, momentum, weights_out, momentum_out, base, momenta, *scratch
-):
-    fragment = 1 - plan[1]
-    buffers, (result, anchors, still, sems, out_sem) = scratch[:4], scratch[4:]
-    sources = (weights, first, second, gradient)
-    copies = []
-    for part in range(2):
-        for i, source in enumerate(sources):
-            copies.append(
-                pltpu.make_async_copy(
-                    source.at[0, fragment, pl.ds(part * 16, 16)], buffers[i].at[part], sems.at[part, i]
-                )
-            )
+def late_swap():
+    return lax.rem(lax.axis_index("fsdp"), 4) == 3
+
+
+def rest_of(part, columns, fragment, factors, sums, gradient, weights, first, second, weights_out, scratch):
+    *buffers, result, sems = scratch
+    rows, cut = pl.ds(part * 16, 16), pl.ds(*columns)
+    here = pl.ds(0, columns[1])
+    copies = [
+        pltpu.make_async_copy(source.at[0, fragment, rows, cut], buffer.at[:, here], sems.at[i])
+        for i, (source, buffer) in enumerate(zip((weights, first, second, gradient), buffers, strict=True))
+    ]
+    for copy in copies:
+        copy.start()
+    factors = adam_factors(sums, factors)
+    for copy in copies:
+        copy.wait()
+
+    def body(k, _):
+        at = columns_of(k)
+        w, m, v, g = (buffer[:, at] for buffer in buffers)
+        result[:, at] = (1.0 - INNER_RATE * WEIGHT_DECAY) * w - adam_change(m, v, g, factors)
+        return 0
+
+    lax.fori_loop(0, columns[1] // STEP, body, 0, unroll=True)
+    out = pltpu.make_async_copy(result.at[:, here], weights_out.at[0, fragment, rows, cut], sems.at[4])
+    out.start()
+    out.wait()
+
+
+def rest_before_kernel(plan, *refs):
+    @pl.when(late_swap())
+    def _():
+        rest_of(0, (0, BEFORE), 1 - plan[1], *refs[:6], refs[6], refs[7:])
+
+
+def rest_beside_kernel(plan, _, anchor, momentum, *refs):
+    fragment = plan[1]
+    args, (weights_out, momentum_out, base, momenta) = refs[:6], refs[7:11]
+    anchors, still, outer_sems, *scratch = refs[11:]
+    copies = [pltpu.make_async_copy(momentum.at[1 - fragment], still, outer_sems.at[2, 0])]
     for part, row in enumerate(halves()):
         rows = pl.ds(row, 16)
-        copies.append(pltpu.make_async_copy(anchor.at[1 - fragment, rows], anchors.at[part], sems.at[part, 4]))
-        copies.append(pltpu.make_async_copy(momentum.at[1 - fragment, rows], momenta.at[part], sems.at[part, 5]))
+        copies.append(pltpu.make_async_copy(anchor.at[fragment, rows], anchors.at[part], outer_sems.at[part, 0]))
+        copies.append(pltpu.make_async_copy(momentum.at[fragment, rows], momenta.at[part], outer_sems.at[part, 1]))
     for copy in copies:
         copy.start()
-    kept = pltpu.make_async_copy(momentum.at[fragment], still, out_sem.at[2])
+
+    @pl.when(jnp.logical_not(late_swap()))
+    def _():
+        rest_of(0, (0, BEFORE), 1 - fragment, *args, weights_out, scratch)
+
+    copies[0].wait()
+    kept = pltpu.make_async_copy(still, momentum_out.at[1 - fragment], outer_sems.at[2, 1])
     kept.start()
-    factors = adam_factors(sums, factors)
-    outs = []
+    whole = momentum.shape[2]
+    rest_of(0, (BEFORE, whole - BEFORE), 1 - fragment, *args, weights_out, scratch)
+    rest_of(1, (0, whole), 1 - fragment, *args, weights_out, scratch)
+    for copy in copies[1:]:
+        copy.wait()
     for part in range(2):
-        for copy in copies[part * 4 : part * 4 + 4]:
-            copy.wait()
-
-        def body(k, _, part=part):
-            at = columns_of(k)
-            w, m, v, g = (buffer[part, :, at] for buffer in buffers)
-            change = adam_change(m, v, g, factors)
-            result[part, :, at] = (1.0 - INNER_RATE * WEIGHT_DECAY) * w - change
-            return 0
-
-        lax.fori_loop(0, result.shape[2] // STEP, body, 0, unroll=True)
-        outs.append(
-            pltpu.make_async_copy(
-                result.at[part], weights_out.at[0, fragment, pl.ds(part * 16, 16)], out_sem.at[part]
-            )
-        )
-        outs[-1].start()
-    kept.wait()
-    outs.append(pltpu.make_async_copy(still, momentum_out.at[fragment], out_sem.at[3]))
-    outs[-1].start()
-    for part in range(2):
-        for copy in copies[8 + 2 * part : 10 + 2 * part]:
-            copy.wait()
 
         def outer(k, _, part=part):
             at = columns_of(k)
@@ -207,9 +221,8 @@
             momenta[part, :, at] = NESTEROV * m
             return 0
 
-        lax.fori_loop(0, result.shape[2] // STEP, outer, 0, unroll=True)
-    for copy in outs:
-        copy.wait()
+        lax.fori_loop(0, base.shape[2] // STEP, outer, 0, unroll=True)
+    kept.wait()
 
 
 def outer_kernel(part, plan, one, two, base, momenta, _, __, weights_out, momentum_out, weight, moment, sems):
@@ -305,34 +318,45 @@
         )(factors, sums, base, firsts, seconds, gradients)
         for part in (0, 1)
     )
+    rest_args = (factors, sums, gradient, local_weights, first_moment, second_moment)
+    half = (16, columns)
+    rest_scratch = [
+        buffer(half, F32),
+        buffer(half, BF16),
+        buffer(half, BF16),
+        buffer(half, BF16),
+        buffer(half, F32),
+        dma((5,)),
+    ]
+    weights_out = shape(local_weights.shape, F32)
+    begun = call(
+        rest_before_kernel,
+        weights_out,
+        [SMEM, VMEM, VMEM] + [HBM] * 4,
+        HBM,
+        rest_scratch,
+        (HIDDEN, HIDDEN),
+    )(chosen, *rest_args)
+    begun = in_hbm(begun)
     summed = call(
         add_kernel,
-        shape((16, columns), BF16),
-        [VMEM, VMEM],
+        shape(half, BF16),
+        [VMEM, VMEM, HBM],
         VMEM,
         [],
         (16 * columns, 96 * columns),
-    )(keep, swap(send, 1))
+    )(keep, swap(send, 1), begun)
     far, theirs = swap(summed, 2), swap(summed, 1)
 
     *outs, outer_base, outer_momenta = call(
-        rest_kernel,
-        [shape(local_weights.shape, F32), shape(anchor.shape, F32), shape(two, F32), shape(two, F32)],
-        [SMEM] + [VMEM] * 3 + [HBM] * 6,
+        rest_beside_kernel,
+        [weights_out, shape(anchor.shape, F32), shape(two, F32), shape(two, F32)],
+        [SMEM, VMEM, HBM, HBM, VMEM, VMEM] + [HBM] * 5,
         [HBM, HBM, VMEM, VMEM],
-        [
-            buffer(two, F32),
-            buffer(two, BF16),
-            buffer(two, BF16),
-            buffer(two, BF16),
-            buffer(two, F32),
-            buffer(two, F32),
-            buffer((rows, columns), F32),
-            dma((2, 6)),
-            dma((4,)),
-        ],
+        [buffer(two, F32), buffer((rows, columns), F32), dma((3, 2)), *rest_scratch],
         (HIDDEN, HIDDEN),
-    )(chosen, factors, sums, summed, gradient, local_weights, first_moment, second_moment, anchor, outer_momentum)
+        {10: 0},
+    )(chosen, summed, anchor, outer_momentum, *rest_args, begun)
 
     far, outer_base = lax.optimization_barrier((far, outer_base))
     for part, one, other in ((1, summed, far), (0, theirs, swap(far, 1))):

time: 39.6 us -> 39.4 us (level)
  the two profiles are of different devices: /device:TPU:33 before, /device:TPU:97 now
where the time goes in v5:
time: 39.4 us; the launch traced here: 39 us
  starting transfers between devices  16.9 us (43%)
  Pallas kernels  14.6 us (37%)
  waiting for transfers between devices  6.2 us (16%)
  between operations  1.36 us (3%)
    all_to_all x1, starting transfers between devices, on_device(): lax.all_to_all(squares.reshape(owners, 1, 128), ('island', 'fsdp'), 0, 0,...  9.51 us
    ppermute x4, starting transfers between devices, swap(): lax.ppermute(x, 'island', [(i, i ^ bit) for i in range(lax.axis_size('isl...  7.36 us
    pallas_call x1, Pallas kernels, on_device(): call(rest_beside_kernel, [weights_out, shape(anchor.shape, F32), shape(tw...  6.4 us
    ppermute x4, waiting for transfers between devices, swap(): lax.ppermute(x, 'island', [(i, i ^ bit) for i in range(lax.axis_size('isl...  4.8 us
    pallas_call x2, Pallas kernels, on_device(): call(functools.partial(outer_kernel, part), [shape(local_weights.shape, F...  2 us
    pallas_call x1, Pallas kernels, on_device(): call(prepare_kernel, [shape(two, F32)] + [shape(two, BF16)] * 3, [SMEM] +...  2 us
    pallas_call x1, Pallas kernels, on_device(): call(squares_kernel, [shape((owners, 128), F32), pltpu.SMEM((2,), jnp.int...  1.98 us
    pallas_call x1, Pallas kernels, on_device(): call(rest_before_kernel, weights_out, [SMEM, VMEM, VMEM] + [HBM] * 4, HBM...  1.48 us
  transfers between devices with their start and end apart: 5, of which 3 were waited for; matrix products, arithmetic and copies ran while one was open for 0% of the time, Pallas kernels for 29%

profile of v5, /device:TPU:97, one launch (start us, length us, event | category | flops | bytes accessed | tf_op | source)
XLA Modules:
  0.0 39.0 jit_solution(5333526738921888421)
XLA Ops:
  0.6 2.0 %shard_map.95 = (f32[64,128]{1,0:T(8,128)}, s32[2]{0:T(128)S(4)}) custom-call(s32[2]{0:T(128)} %plan.1, bf16[1,2,32,7168]{3,2,1,0:T(8,128)(2,1)} %refs_2_.3), custom_call_target="tpu_custom_call" | custom-call | flops 917504 | bytes 917504 | tf_op jit(solution)/shard_map/pallas_call | solution.py:289
  2.6 9.5 %all-to-all-start = ((f32[64,1,128]{2,1,0:T(1,128)}), f32[64,1,128]{2,1,0:T(1,128)S(1)}, u32[]{:S(2)}, u32[]{:S(2)}) async-start(f32[64,1,128]{2,1,0:T(1,128)} %bitcast.1), calls=%async_computation | async-start | bytes 65536 | tf_op jit(solution)/shard_map/all_to_all | solution.py:298
  12.8 2.0 %shard_map.97 = (f32[2,16,7168]{2,1,0:T(8,128)S(1)}, bf16[2,16,7168]{2,1,0:T(8,128)(2,1)S(1)}, bf16[2,16,7168]{2,1,0:T(8,128)(2,1)S(1)}, bf16[2,16,7168]{2,1,0:T(8,128)(2,1)S(1)}) custom-call(s32[2]{0:T(128)S(4)} %get-tuple-element.18.plan, f32[1,2,32,7168]{3,2,1,0:T(8,128)} %refs_3_.3, bf16[1,2,32,7168]{3,2,1,0:T(8,128)(2,1)} %refs_4_.3, ...), custom_call_target="tpu_custom_call" | custom-call | flops 40000000 | bytes 40000000 | tf_op jit(solution)/shard_map/pallas_call | solution.py:301
  14.8 1.4 %all-to-all-done = f32[64,1,128]{2,1,0:T(1,128)S(1)} async-done(((f32[64,1,128]{2,1,0:T(1,128)}), f32[64,1,128]{2,1,0:T(1,128)S(1)}, u32[]{:S(2)}, u32[]{:S(2)}) %all-to-all-start) | async-done | bytes 32800 | tf_op jit(solution)/shard_map/all_to_all | solution.py:298
  16.2 0.3 shard_map.99
  16.6 1.5 %collective-permute-start = (bf16[16,7168]{1,0:T(8,128)(2,1)S(1)}, bf16[16,7168]{1,0:T(8,128)(2,1)S(1)}, u32[]{:S(2)}, u32[]{:S(2)}) collective-permute-start(bf16[16,7168]{1,0:T(8,128)(2,1)S(1)} %shard_map.99), channel_id=1, source_target_pairs={{0,64},{64,0},{128,192},{192,128},{1,65},{65,1},{129,193},{193,129... | collective-permute-start | bytes 688136 | tf_op jit(solution)/shard_map/ppermute | solution.py:269
  18.0 0.3 shard_map.98.one
  18.4 1.5 %shard_map.100._.refs_6_ = f32[1,2,32,7168]{3,2,1,0:T(8,128)} custom-call(s32[2]{0:T(128)S(4)} %get-tuple-element.18.plan, f32[8,128]{1,0:T(8,128)S(1)} %shard_map.96.factors.refs_0_, f32[64,128]{1,0:T(8,128)S(1)} %bitcast.6, bf16[1,2,32,7168]{3,2,1,0:T(8,128)(2,1)} %refs_2_.3, f32[1,2,32,7168]{3,2,1,0:T(8,128)} %refs_3_.3, ...), custom_call_target="tpu_custom_call" | custom-call | flops 40000000 | bytes 40000000 | tf_op jit(solution)/shard_map/pallas_call | solution.py:332
  19.9 0.0 collective-permute-done.two
  19.9 0.1 shard_map.101._.one
  20.0 4.7 %collective-permute-start.2 = (bf16[16,7168]{1,0:T(8,128)(2,1)S(1)}, bf16[16,7168]{1,0:T(8,128)(2,1)S(1)}, u32[]{:S(2)}, u32[]{:S(2)}) collective-permute-start(bf16[16,7168]{1,0:T(8,128)(2,1)S(1)} %shard_map.101._.one), channel_id=1, source_target_pairs={{0,128},{64,192},{128,0},{192,64},{1,129},{65,193},{129,1},{193,65... | collective-permute-start | bytes 688136 | tf_op jit(solution)/shard_map/ppermute | solution.py:269
  24.7 0.3 collective-permute-start.1
  25.0 6.4 %shard_map.102 = (f32[1,2,32,7168]{3,2,1,0:T(8,128)}, f32[2,32,7168]{2,1,0:T(8,128)}, f32[2,16,7168]{2,1,0:T(8,128)S(1)}, f32[2,16,7168]{2,1,0:T(8,128)S(1)}) custom-call(s32[2]{0:T(128)S(4)} %get-tuple-element.18.plan, bf16[16,7168]{1,0:T(8,128)(2,1)S(1)} %shard_map.101._.one, f32[2,32,7168]{2,1,0:T(8,128)} %anchor.3, ...), custom_call_target="tpu_custom_call", output_to_operand_aliasing={{0}: (10, {})} | custom-call | flops 40000000 | bytes 40000000 | tf_op jit(solution)/shard_map/pallas_call | solution.py:351
  31.4 4.7 %collective-permute-done.2.two = bf16[16,7168]{1,0:T(8,128)(2,1)S(1)} collective-permute-done((bf16[16,7168]{1,0:T(8,128)(2,1)S(1)}, bf16[16,7168]{1,0:T(8,128)(2,1)S(1)}, u32[]{:S(2)}, u32[]{:S(2)}) %collective-permute-start.2) | collective-permute-done | bytes 229408 | tf_op jit(solution)/shard_map/ppermute | solution.py:269
  36.1 0.8 %collective-permute-start.3 = (bf16[16,7168]{1,0:T(8,128)(2,1)S(1)}, bf16[16,7168]{1,0:T(8,128)(2,1)S(1)}, u32[]{:S(2)}, u32[]{:S(2)}) collective-permute-start(bf16[16,7168]{1,0:T(8,128)(2,1)S(1)} %collective-permute-done.2.two), channel_id=1, source_target_pairs={{0,64},{64,0},{128,192},{192,128},{1,65},{65,1},{129,193},{193,129... | collective-permute-start | bytes 688136 | tf_op jit(solution)/shard_map/ppermute | solution.py:269
  36.9 1.0 %shard_map.103 = (f32[1,2,32,7168]{3,2,1,0:T(8,128)}, f32[2,32,7168]{2,1,0:T(8,128)}) custom-call(s32[2]{0:T(128)S(4)} %get-tuple-element.18.plan, bf16[16,7168]{1,0:T(8,128)(2,1)S(1)} %shard_map.101._.one, bf16[16,7168]{1,0:T(8,128)(2,1)S(1)} %collective-permute-done.2.two, ...), custom_call_target="tpu_custom_call", output_to_operand_aliasing={{0}: (5, {}), {1}: (6, {})} | custom-call | flops 40000000 | bytes 40000000 | tf_op jit(solution)/shard_map/pallas_call | solution.py:363
  37.9 0.0 collective-permute-done.1.one
  37.9 0.1 collective-permute-done.3.two
  38.0 1.0 %shard_map.104 = (f32[1,2,32,7168]{3,2,1,0:T(8,128)}, f32[2,32,7168]{2,1,0:T(8,128)}) custom-call(s32[2]{0:T(128)S(4)} %get-tuple-element.18.plan, bf16[16,7168]{1,0:T(8,128)(2,1)S(1)} %collective-permute-done.1.one, bf16[16,7168]{1,0:T(8,128)(2,1)S(1)} %collective-permute-done.3.two, ...), custom_call_target="tpu_custom_call", output_to_operand_aliasing={{0}: (5, {}), {1}: (6, {})} | custom-call | flops 1 | bytes 1 | tf_op jit(solution)/shard_map/pallas_call | solution.py:363
  (1 shorter events, 0.0 us)
Async XLA Ops:
  2.6 13.6 %all-to-all-start = ((f32[64,1,128]{2,1,0:T(1,128)}), f32[64,1,128]{2,1,0:T(1,128)S(1)}, u32[]{:S(2)}, u32[]{:S(2)}) async-start(f32[64,1,128]{2,1,0:T(1,128)} %bitcast.1), calls=%async_computation | async-start | bytes 65536 | tf_op jit(solution)/shard_map/all_to_all | solution.py:298
  16.6 3.3 %collective-permute-start = (bf16[16,7168]{1,0:T(8,128)(2,1)S(1)}, bf16[16,7168]{1,0:T(8,128)(2,1)S(1)}, u32[]{:S(2)}, u32[]{:S(2)}) collective-permute-start(bf16[16,7168]{1,0:T(8,128)(2,1)S(1)} %shard_map.99), channel_id=1, source_target_pairs={{0,64},{64,0},{128,192},{192,128},{1,65},{65,1},{129,193},{193,129... | collective-permute-start | bytes 688136 | tf_op jit(solution)/shard_map/ppermute | solution.py:269
  20.0 16.1 %collective-permute-start.2 = (bf16[16,7168]{1,0:T(8,128)(2,1)S(1)}, bf16[16,7168]{1,0:T(8,128)(2,1)S(1)}, u32[]{:S(2)}, u32[]{:S(2)}) collective-permute-start(bf16[16,7168]{1,0:T(8,128)(2,1)S(1)} %shard_map.101._.one), channel_id=1, source_target_pairs={{0,128},{64,192},{128,0},{192,64},{1,129},{65,193},{129,1},{193,65... | collective-permute-start | bytes 688136 | tf_op jit(solution)/shard_map/ppermute | solution.py:269
  24.7 13.3 %collective-permute-start.1 = (bf16[16,7168]{1,0:T(8,128)(2,1)S(1)}, bf16[16,7168]{1,0:T(8,128)(2,1)S(1)}, u32[]{:S(2)}, u32[]{:S(2)}) collective-permute-start(bf16[16,7168]{1,0:T(8,128)(2,1)S(1)} %shard_map.101._.one), channel_id=1, source_target_pairs={{0,64},{64,0},{128,192},{192,128},{1,65},{65,1},{129,193},{193,129... | collective-permute-start | bytes 688136 | tf_op jit(solution)/shard_map/ppermute | solution.py:269
  36.1 2.0 %collective-permute-start.3 = (bf16[16,7168]{1,0:T(8,128)(2,1)S(1)}, bf16[16,7168]{1,0:T(8,128)(2,1)S(1)}, u32[]{:S(2)}, u32[]{:S(2)}) collective-permute-start(bf16[16,7168]{1,0:T(8,128)(2,1)S(1)} %collective-permute-done.2.two), channel_id=1, source_target_pairs={{0,64},{64,0},{128,192},{192,128},{1,65},{65,1},{129,193},{193,129... | collective-permute-start | bytes 688136 | tf_op jit(solution)/shard_map/ppermute | solution.py:269

commit v6 on v5

--- a/solution.py
+++ b/solution.py
@@ -153,7 +153,7 @@
 
 
 def late_swap():
-    return lax.rem(lax.axis_index("fsdp"), 4) == 3
+    return jnp.logical_and(lax.rem(lax.axis_index("fsdp"), 4) == 3, lax.axis_index("island") < 2)
 
 
 def rest_of(part, columns, fragment, factors, sums, gradient, weights, first, second, weights_out, scratch):

time: 39.4 us -> 39.4 us (level)
  starting transfers between devices: 16.9 us -> 16.5 us
where the time goes in v6:
time: 39.4 us; the launch traced here: 39 us
  starting transfers between devices  16.5 us (42%)
  Pallas kernels  14.6 us (37%)
  waiting for transfers between devices  6.58 us (17%)
  between operations  1.36 us (3%)
    all_to_all x1, starting transfers between devices, on_device(): lax.all_to_all(squares.reshape(owners, 1, 128), ('island', 'fsdp'), 0, 0,...  9.51 us
    ppermute x4, starting transfers between devices, swap(): lax.ppermute(x, 'island', [(i, i ^ bit) for i in range(lax.axis_size('isl...  6.98 us
    pallas_call x1, Pallas kernels, on_device(): call(rest_beside_kernel, [weights_out, shape(anchor.shape, F32), shape(tw...  6.4 us
    ppermute x4, waiting for transfers between devices, swap(): lax.ppermute(x, 'island', [(i, i ^ bit) for i in range(lax.axis_size('isl...  5.18 us
    pallas_call x2, Pallas kernels, on_device(): call(functools.partial(outer_kernel, part), [shape(local_weights.shape, F...  2 us
    pallas_call x1, Pallas kernels, on_device(): call(prepare_kernel, [shape(two, F32)] + [shape(two, BF16)] * 3, [SMEM] +...  2 us
    pallas_call x1, Pallas kernels, on_device(): call(squares_kernel, [shape((owners, 128), F32), pltpu.SMEM((2,), jnp.int...  1.98 us
    pallas_call x1, Pallas kernels, on_device(): call(rest_before_kernel, weights_out, [SMEM, VMEM, VMEM] + [HBM] * 4, HBM...  1.48 us
  transfers between devices with their start and end apart: 5, of which 3 were waited for; matrix products, arithmetic and copies ran while one was open for 0% of the time, Pallas kernels for 29%

profile of v6, /device:TPU:97, one launch (start us, length us, event | category | flops | bytes accessed | tf_op | source)
XLA Modules:
  0.0 39.0 jit_solution(9642379004722213585)
XLA Ops:
  0.6 2.0 %shard_map.95 = (f32[64,128]{1,0:T(8,128)}, s32[2]{0:T(128)S(4)}) custom-call(s32[2]{0:T(128)} %plan.1, bf16[1,2,32,7168]{3,2,1,0:T(8,128)(2,1)} %refs_2_.3), custom_call_target="tpu_custom_call" | custom-call | flops 917504 | bytes 917504 | tf_op jit(solution)/shard_map/pallas_call | solution.py:289
  2.6 9.5 %all-to-all-start = ((f32[64,1,128]{2,1,0:T(1,128)}), f32[64,1,128]{2,1,0:T(1,128)S(1)}, u32[]{:S(2)}, u32[]{:S(2)}) async-start(f32[64,1,128]{2,1,0:T(1,128)} %bitcast.1), calls=%async_computation | async-start | bytes 65536 | tf_op jit(solution)/shard_map/all_to_all | solution.py:298
  12.8 2.0 %shard_map.97 = (f32[2,16,7168]{2,1,0:T(8,128)S(1)}, bf16[2,16,7168]{2,1,0:T(8,128)(2,1)S(1)}, bf16[2,16,7168]{2,1,0:T(8,128)(2,1)S(1)}, bf16[2,16,7168]{2,1,0:T(8,128)(2,1)S(1)}) custom-call(s32[2]{0:T(128)S(4)} %get-tuple-element.18.plan, f32[1,2,32,7168]{3,2,1,0:T(8,128)} %refs_3_.3, bf16[1,2,32,7168]{3,2,1,0:T(8,128)(2,1)} %refs_4_.3, ...), custom_call_target="tpu_custom_call" | custom-call | flops 40000000 | bytes 40000000 | tf_op jit(solution)/shard_map/pallas_call | solution.py:301
  14.8 1.4 %all-to-all-done = f32[64,1,128]{2,1,0:T(1,128)S(1)} async-done(((f32[64,1,128]{2,1,0:T(1,128)}), f32[64,1,128]{2,1,0:T(1,128)S(1)}, u32[]{:S(2)}, u32[]{:S(2)}) %all-to-all-start) | async-done | bytes 32800 | tf_op jit(solution)/shard_map/all_to_all | solution.py:298
  16.2 0.3 shard_map.99
  16.6 1.5 %collective-permute-start = (bf16[16,7168]{1,0:T(8,128)(2,1)S(1)}, bf16[16,7168]{1,0:T(8,128)(2,1)S(1)}, u32[]{:S(2)}, u32[]{:S(2)}) collective-permute-start(bf16[16,7168]{1,0:T(8,128)(2,1)S(1)} %shard_map.99), channel_id=1, source_target_pairs={{0,64},{64,0},{128,192},{192,128},{1,65},{65,1},{129,193},{193,129... | collective-permute-start | bytes 688136 | tf_op jit(solution)/shard_map/ppermute | solution.py:269
  18.0 0.3 shard_map.98.one
  18.4 1.5 %shard_map.100._.refs_6_ = f32[1,2,32,7168]{3,2,1,0:T(8,128)} custom-call(s32[2]{0:T(128)S(4)} %get-tuple-element.18.plan, f32[8,128]{1,0:T(8,128)S(1)} %shard_map.96.factors.refs_0_, f32[64,128]{1,0:T(8,128)S(1)} %bitcast.6, bf16[1,2,32,7168]{3,2,1,0:T(8,128)(2,1)} %refs_2_.3, f32[1,2,32,7168]{3,2,1,0:T(8,128)} %refs_3_.3, ...), custom_call_target="tpu_custom_call" | custom-call | flops 40000000 | bytes 40000000 | tf_op jit(solution)/shard_map/pallas_call | solution.py:332
  19.9 0.0 collective-permute-done.two
  19.9 0.1 shard_map.101._.one
  20.0 4.0 %collective-permute-start.2 = (bf16[16,7168]{1,0:T(8,128)(2,1)S(1)}, bf16[16,7168]{1,0:T(8,128)(2,1)S(1)}, u32[]{:S(2)}, u32[]{:S(2)}) collective-permute-start(bf16[16,7168]{1,0:T(8,128)(2,1)S(1)} %shard_map.101._.one), channel_id=1, source_target_pairs={{0,128},{64,192},{128,0},{192,64},{1,129},{65,193},{129,1},{193,65... | collective-permute-start | bytes 688136 | tf_op jit(solution)/shard_map/ppermute | solution.py:269
  23.9 0.7 %collective-permute-start.1 = (bf16[16,7168]{1,0:T(8,128)(2,1)S(1)}, bf16[16,7168]{1,0:T(8,128)(2,1)S(1)}, u32[]{:S(2)}, u32[]{:S(2)}) collective-permute-start(bf16[16,7168]{1,0:T(8,128)(2,1)S(1)} %shard_map.101._.one), channel_id=1, source_target_pairs={{0,64},{64,0},{128,192},{192,128},{1,65},{65,1},{129,193},{193,129... | collective-permute-start | bytes 688136 | tf_op jit(solution)/shard_map/ppermute | solution.py:269
  24.6 6.4 %shard_map.102 = (f32[1,2,32,7168]{3,2,1,0:T(8,128)}, f32[2,32,7168]{2,1,0:T(8,128)}, f32[2,16,7168]{2,1,0:T(8,128)S(1)}, f32[2,16,7168]{2,1,0:T(8,128)S(1)}) custom-call(s32[2]{0:T(128)S(4)} %get-tuple-element.18.plan, bf16[16,7168]{1,0:T(8,128)(2,1)S(1)} %shard_map.101._.one, f32[2,32,7168]{2,1,0:T(8,128)} %anchor.3, ...), custom_call_target="tpu_custom_call", output_to_operand_aliasing={{0}: (10, {})} | custom-call | flops 40000000 | bytes 40000000 | tf_op jit(solution)/shard_map/pallas_call | solution.py:351
  31.0 5.1 %collective-permute-done.2.two = bf16[16,7168]{1,0:T(8,128)(2,1)S(1)} collective-permute-done((bf16[16,7168]{1,0:T(8,128)(2,1)S(1)}, bf16[16,7168]{1,0:T(8,128)(2,1)S(1)}, u32[]{:S(2)}, u32[]{:S(2)}) %collective-permute-start.2) | collective-permute-done | bytes 229408 | tf_op jit(solution)/shard_map/ppermute | solution.py:269
  36.1 0.8 %collective-permute-start.3 = (bf16[16,7168]{1,0:T(8,128)(2,1)S(1)}, bf16[16,7168]{1,0:T(8,128)(2,1)S(1)}, u32[]{:S(2)}, u32[]{:S(2)}) collective-permute-start(bf16[16,7168]{1,0:T(8,128)(2,1)S(1)} %collective-permute-done.2.two), channel_id=1, source_target_pairs={{0,64},{64,0},{128,192},{192,128},{1,65},{65,1},{129,193},{193,129... | collective-permute-start | bytes 688136 | tf_op jit(solution)/shard_map/ppermute | solution.py:269
  36.9 1.0 %shard_map.103 = (f32[1,2,32,7168]{3,2,1,0:T(8,128)}, f32[2,32,7168]{2,1,0:T(8,128)}) custom-call(s32[2]{0:T(128)S(4)} %get-tuple-element.18.plan, bf16[16,7168]{1,0:T(8,128)(2,1)S(1)} %shard_map.101._.one, bf16[16,7168]{1,0:T(8,128)(2,1)S(1)} %collective-permute-done.2.two, ...), custom_call_target="tpu_custom_call", output_to_operand_aliasing={{0}: (5, {}), {1}: (6, {})} | custom-call | flops 40000000 | bytes 40000000 | tf_op jit(solution)/shard_map/pallas_call | solution.py:363
  37.9 0.0 collective-permute-done.1.one
  37.9 0.1 collective-permute-done.3.two
  38.0 1.0 %shard_map.104 = (f32[1,2,32,7168]{3,2,1,0:T(8,128)}, f32[2,32,7168]{2,1,0:T(8,128)}) custom-call(s32[2]{0:T(128)S(4)} %get-tuple-element.18.plan, bf16[16,7168]{1,0:T(8,128)(2,1)S(1)} %collective-permute-done.1.one, bf16[16,7168]{1,0:T(8,128)(2,1)S(1)} %collective-permute-done.3.two, ...), custom_call_target="tpu_custom_call", output_to_operand_aliasing={{0}: (5, {}), {1}: (6, {})} | custom-call | flops 1 | bytes 1 | tf_op jit(solution)/shard_map/pallas_call | solution.py:363
  (1 shorter events, 0.0 us)
Async XLA Ops:
  2.6 13.6 %all-to-all-start = ((f32[64,1,128]{2,1,0:T(1,128)}), f32[64,1,128]{2,1,0:T(1,128)S(1)}, u32[]{:S(2)}, u32[]{:S(2)}) async-start(f32[64,1,128]{2,1,0:T(1,128)} %bitcast.1), calls=%async_computation | async-start | bytes 65536 | tf_op jit(solution)/shard_map/all_to_all | solution.py:298
  16.6 3.3 %collective-permute-start = (bf16[16,7168]{1,0:T(8,128)(2,1)S(1)}, bf16[16,7168]{1,0:T(8,128)(2,1)S(1)}, u32[]{:S(2)}, u32[]{:S(2)}) collective-permute-start(bf16[16,7168]{1,0:T(8,128)(2,1)S(1)} %shard_map.99), channel_id=1, source_target_pairs={{0,64},{64,0},{128,192},{192,128},{1,65},{65,1},{129,193},{193,129... | collective-permute-start | bytes 688136 | tf_op jit(solution)/shard_map/ppermute | solution.py:269
  20.0 16.1 %collective-permute-start.2 = (bf16[16,7168]{1,0:T(8,128)(2,1)S(1)}, bf16[16,7168]{1,0:T(8,128)(2,1)S(1)}, u32[]{:S(2)}, u32[]{:S(2)}) collective-permute-start(bf16[16,7168]{1,0:T(8,128)(2,1)S(1)} %shard_map.101._.one), channel_id=1, source_target_pairs={{0,128},{64,192},{128,0},{192,64},{1,129},{65,193},{129,1},{193,65... | collective-permute-start | bytes 688136 | tf_op jit(solution)/shard_map/ppermute | solution.py:269
  23.9 14.0 %collective-permute-start.1 = (bf16[16,7168]{1,0:T(8,128)(2,1)S(1)}, bf16[16,7168]{1,0:T(8,128)(2,1)S(1)}, u32[]{:S(2)}, u32[]{:S(2)}) collective-permute-start(bf16[16,7168]{1,0:T(8,128)(2,1)S(1)} %shard_map.101._.one), channel_id=1, source_target_pairs={{0,64},{64,0},{128,192},{192,128},{1,65},{65,1},{129,193},{193,129... | collective-permute-start | bytes 688136 | tf_op jit(solution)/shard_map/ppermute | solution.py:269
  36.1 2.0 %collective-permute-start.3 = (bf16[16,7168]{1,0:T(8,128)(2,1)S(1)}, bf16[16,7168]{1,0:T(8,128)(2,1)S(1)}, u32[]{:S(2)}, u32[]{:S(2)}) collective-permute-start(bf16[16,7168]{1,0:T(8,128)(2,1)S(1)} %collective-permute-done.2.two), channel_id=1, source_target_pairs={{0,64},{64,0},{128,192},{192,128},{1,65},{65,1},{129,193},{193,129... | collective-permute-start | bytes 688136 | tf_op jit(solution)/shard_map/ppermute | solution.py:269
